TPU v7x, 128 devices: a whole 4x4x4 slice. The times are simulated.
128 devices in a mesh: dap: 32 (over z, x, core), rep: 4 (over y).
Axes of the slice: x: 4, y: 4, z: 4, core: 2. Of those that a mesh axis runs over, the one named last changes fastest.
Arguments:
- alignment_features: bfloat16 [256, 2048, 256], P('dap', 'rep'), may hold values from -6 to 6
- presence_indicator: bfloat16 [256, 2048], P('dap', 'rep'), may hold values from 0 to 1, as said below
- genuine_position_indicator: int32 [2048], replicated, may hold values from 0 to 1, as said below
- standardizer_scale: float32 [256], replicated, may hold values from 0.1 to 1.9
- standardizer_offset: float32 [256], replicated, may hold values from -3 to 3
- first_factor_matrix: bfloat16 [256, 32], replicated, may hold values from -0.375 to 0.375
- first_factor_offset: float32 [32], replicated, may hold values from -3 to 3
- second_factor_matrix: bfloat16 [256, 32], replicated, may hold values from -0.375 to 0.375
- second_factor_offset: float32 [32], replicated, may hold values from -3 to 3
- final_projection_matrix: bfloat16 [1024, 128], replicated, may hold values from -1.5 to 1.5
- final_projection_offset: float32 [128], replicated, may hold values from -3 to 3
Outputs:
- pair_update: bfloat16 [2048, 2048, 128], P('dap', 'rep')
Inputs may be any that keep to these rules, and one draw needn't show every extreme that they name: `genuine_position_indicator`: 1 for the first residues up to a drawn length and 0 after it; some residues are padding. `presence_indicator`: 0 for absent entries, a real weight otherwise.
All inputs are finite; a program needn't handle non-finite values.
Results may differ from a plain program's by a relative error of at most 0.0054.
Values may be sent and summed in bfloat16 or wider, within the bound.
No kernel may reach another device: no remote copies, remote signals or barrier semaphores. Data moves between devices by JAX's collectives and lax.ppermute only.
A program may use at most 128 MiB of HBM per device.

v0:
```python
import math

import jax
import jax.numpy as jnp
from jax import lax
from jax.sharding import PartitionSpec as P


def standardize_features(values, standardizer_scale, standardizer_offset):
    values = values.astype(jnp.float32)
    average = jnp.mean(values, axis=-1, keepdims=True)
    centred = values - average
    variance = jnp.mean(centred * centred, axis=-1, keepdims=True)
    return (
        centred * lax.rsqrt(variance + 1e-05) * standardizer_scale + standardizer_offset
    ).astype(jnp.bfloat16)


def project(standardized_alignment, weight, shift, kept_mask):
    seqs_here, residues, feature_total = standardized_alignment.shape
    result = jnp.dot(
        standardized_alignment.reshape(seqs_here * residues, feature_total),
        weight,
        preferred_element_type=jnp.float32,
    )
    result = result.reshape(seqs_here, residues, -1)
    return ((result + shift) * kept_mask[..., None].astype(jnp.float32)).astype(jnp.bfloat16)


def per_device(
    alignment_features,
    presence_indicator,
    genuine_position_indicator,
    standardizer_scale,
    standardizer_offset,
    first_factor_matrix,
    first_factor_offset,
    second_factor_matrix,
    second_factor_offset,
    final_projection_matrix,
    final_projection_offset,
):
    homologs_on_device, column_count, feature_total = alignment_features.shape
    proj_width = first_factor_matrix.shape[1]
    out_width = final_projection_matrix.shape[1]
    column_offset = lax.axis_index("rep") * column_count
    pad_columns = lax.dynamic_slice_in_dim(
        genuine_position_indicator, column_offset, column_count, 0
    )
    kept_mask = (
        presence_indicator.astype(jnp.float32) * pad_columns[None, :].astype(jnp.float32)
    ).astype(jnp.bfloat16)
    standardized_alignment = standardize_features(
        alignment_features, standardizer_scale, standardizer_offset
    )
    right = project(standardized_alignment, second_factor_matrix, second_factor_offset, kept_mask)
    right = jnp.transpose(right, (0, 2, 1)).reshape(homologs_on_device, proj_width * column_count)
    right_all, kept_columns = (
        lax.all_gather(right, "dap", axis=0, tiled=True),
        lax.all_gather(kept_mask, "dap", axis=0, tiled=True),
    )
    raw_flat = alignment_features.reshape(homologs_on_device, column_count * feature_total)
    raw_wide, kept_wide = (
        lax.all_gather(raw_flat, "rep", axis=1, tiled=True),
        lax.all_gather(kept_mask, "rep", axis=1, tiled=True),
    )
    raw_rows, kept_rows = (
        lax.all_to_all(raw_wide, "dap", split_axis=1, concat_axis=0, tiled=True),
        lax.all_to_all(kept_wide, "dap", split_axis=1, concat_axis=0, tiled=True),
    )
    row_total = kept_rows.shape[1]
    normed_rows = standardize_features(
        raw_rows.reshape(-1, row_total, feature_total), standardizer_scale, standardizer_offset
    )
    left_rows = project(normed_rows, first_factor_matrix, first_factor_offset, kept_rows).reshape(
        -1, row_total * proj_width
    )
    row_total = kept_rows.shape[1]
    counts = lax.dot_general(
        kept_rows, kept_columns, (((0,), (0,)), ((), ())), preferred_element_type=jnp.float32
    )
    block_rows = math.gcd(row_total, 8)

    def one_block(offset):
        left_block = lax.dynamic_slice_in_dim(
            left_rows, offset * proj_width, block_rows * proj_width, 1
        )
        outer = lax.dot_general(
            left_block, right_all, (((0,), (0,)), ((), ())), preferred_element_type=jnp.float32
        )
        outer = outer.astype(jnp.bfloat16).reshape(
            block_rows, proj_width * proj_width, column_count
        )
        projected = lax.dot_general(
            outer,
            final_projection_matrix,
            (((1,), (0,)), ((), ())),
            preferred_element_type=jnp.float32,
        )
        count_block = lax.dynamic_slice_in_dim(counts, offset, block_rows, 0)
        return (
            (projected + final_projection_offset) / jnp.maximum(count_block, 1.0)[..., None]
        ).astype(jnp.bfloat16)

    offsets = jnp.arange(row_total // block_rows) * block_rows
    blocks = lax.map(one_block, offsets)
    return blocks.reshape(row_total, column_count, out_width)


def solution(mesh):
    in_specs = (P("dap", "rep", None), P("dap", "rep"), P(), P(), P(), P(), P(), P(), P(), P(), P())
    out_specs = P("dap", "rep", None)
    return jax.shard_map(
        per_device, mesh=mesh, in_specs=in_specs, out_specs=out_specs, check_vma=False
    )
```

profile of v0, /device:TPU:0, one launch (start us, length us, event | category | flops | bytes accessed | tf_op | source)
XLA Modules:
  0.0 569.9 jit_solution(10024543289200866612)
XLA Ops:
  6.6 0.0 all-gather.3.cloned.1.call-start
  6.6 4.2 copy.24
  10.8 0.0 all-gather.3.cloned.1.call-update
  10.9 0.0 all-gather.5.cloned.1.call-start
  10.9 0.8 dynamic-slice_convert_fusion
  11.7 2.2 convert_reduce_fusion
  13.9 1.3 fusion.8
  15.3 1.5 fusion.23
  16.9 0.9 copy.26
  17.7 0.0 all-gather.5.cloned.1.call-update
  17.8 12.5 %all_gather.13 = bf16[8,2048]{1,0:T(8,128)(2,1)S(1)} all-gather(bf16[8,512]{1,0:T(8,128)(2,1)S(1)} %get-tuple-element.81), channel_id=1, replica_groups=mesh['dap'=32,'rep'=4] {'rep'}, dimensions={1}, use_global_device_ids=true | all-gather | bytes 40960 | tf_op jit(solution)/shard_map/all_gather | solution.py:65
  30.3 0.1 all_to_all.24
  30.4 0.1 reshape.108
  30.5 15.4 %all_to_all.29 = bf16[32,2,256]{2,1,0:T(2,128)(2,1)S(1)} all-to-all(bf16[32,2,256]{2,1,0:T(2,128)(2,1)S(1)} %reshape.108), channel_id=1, replica_groups=mesh['dap'=32,'rep'=4] {'dap'}, dimensions={0} | all-to-all | bytes 65536 | tf_op jit(solution)/shard_map/all_to_all | solution.py:69
  45.9 50.7 %all-gather.3.cloned.1.call-done = bf16[8,524288]{1,0:T(8,128)(2,1)} async-done(((bf16[8,131072]{1,0:T(8,128)(2,1)}), bf16[8,524288]{1,0:T(8,128)(2,1)}) %all-gather.3.cloned.1.call-update) | async-done | bytes 8388624 | tf_op jit(solution)/shard_map/all_gather | solution.py:64
  96.7 7.4 %all-to-all-start = ((bf16[8,32,16384]{2,0,1:T(8,128)(2,1)}), bf16[8,32,16384]{2,0,1:T(8,128)(2,1)}, u32[]{:S(2)}, u32[]{:S(2)}) async-start(bf16[8,32,16384]{2,0,1:T(8,128)(2,1)} %bitcast.60), calls=%async_computation | async-start | bytes 16777216 | tf_op jit(solution)/shard_map/all_to_all | solution.py:68
  104.1 135.1 %all_gather.15 = bf16[256,512]{1,0:T(8,128)(2,1)S(1)} all-gather(bf16[8,512]{1,0:T(8,128)(2,1)S(1)} %get-tuple-element.81), channel_id=1, replica_groups=mesh['dap'=32,'rep'=4] {'dap'}, dimensions={0}, use_global_device_ids=true | all-gather | bytes 270336 | tf_op jit(solution)/shard_map/all_gather | solution.py:60
  239.2 0.1 reshape.109
  239.3 0.1 copy.18
  239.4 0.2 fusion.26
  239.6 0.0 all-to-all-done
  239.6 11.1 %convert_element_type.75 = f32[8,32,16384]{2,0,1:T(8,128)} convert(bf16[8,32,16384]{2,0,1:T(8,128)(2,1)} %all-to-all-done) | non-fusion elementwise | flops 4194304 | bytes 25165824 | tf_op jit(solution)/shard_map/convert_element_type | solution.py:10
  250.7 15.8 %copy.25 = f32[32,8,64,256]{3,2,1,0:T(8,128)} copy(f32[32,8,64,256]{3,1,2,0:T(8,128)} %bitcast.58) | data formatting | bytes 33554432
  266.5 8.0 %reduce_sum.36 = f32[256,64]{1,0:T(8,128)S(1)} reduce(f32[256,64,256]{2,1,0:T(8,128)} %bitcast.55, f32[]{:T(128)} %constant.26.clone.1), dimensions={2}, to_apply=%region_0.0 | reduce | flops 4177920 | bytes 16842756 | tf_op jit(solution)/shard_map/reduce_sum | solution.py:11
  274.5 9.5 %multiply_reduce_fusion = f32[256,64]{1,0:T(8,128)S(1)} fusion(f32[256,64,256]{2,1,0:T(8,128)} %bitcast.56, f32[256,64]{1,0:T(8,128)S(1)} %broadcast_multiply_fusion), kind=kLoop, calls=%fused_computation.9 | loop fusion | flops 12566528 | bytes 16908288 | tf_op jit(solution)/shard_map/reduce_sum | solution.py:13
  284.1 1.1 copy-done.2
  285.2 8.7 %fusion.5 = f32[256,64,32]{1,2,0:T(8,128)} fusion(f32[256,64,256]{2,1,0:T(8,128)S(1)} %bitcast.57, f32[256]{0:T(256)S(1)} %copy-done.5, f32[256]{0:T(256)S(1)} %copy-done.6, f32[256,64]{1,0:T(8,128)S(1)} %add_rsqrt_fusion, f32[256,64]{1,0:T(8,128)S(1)} %broadcast_multiply_fusion, bf16[256,32]{0,1:T(8,128)(2,1)S(1)} %copy-done), kind=kOutput, calls=%fused_computation.10 | convolution fusion | flops 289406976 | bytes 19023872 | tf_op jit(solution)/shard_map/dot_general | solution.py:21
  293.9 4.5 copy.22
  298.4 0.4 multiply_convert_fusion
  298.8 0.0 all-gather.5.cloned.1.call-done
  298.8 263.5 %while.10 = (s32[]{:T(128)}, bf16[8,8,512,128]{3,2,1,0:T(8,128)(2,1)}, s32[8]{0:T(128)S(1)}, bf16[256,2048]{0,1:T(8,128)(2,1)S(1)}, bf16[256,16384]{1,0:T(8,128)...) while((s32[]{:T(128)}, ...), condition=%wide.region_5.6_spmd, body=%wide.region_4.5_spmd.sunk | while | flops 3226996736 | bytes 44483832 | solution.py:106
  299.1 0.6 dynamic_slice.23
  300.3 9.0 %convolution_convert_fusion.2 = bf16[256,16384]{1,0:T(8,128)(2,1)} fusion(bf16[256,16384]{1,0:T(8,128)(2,1)} %get-tuple-element.161, bf16[256,2048]{0,1:T(8,128)(2,1)S(1)} %get-tuple-element.160, s32[]{:T(128)S(6)} %select_n.12), kind=kOutput, calls=%fused_computation.clone.1 | convolution fusion | flops 2151677952 | bytes 16908292 | tf_op jit(solution)/shard_map/while/body/eval_jaxpr/dot_general | solution.py:88
  309.3 13.6 %reshape.111 = bf16[8,1024,512]{2,1,0:T(8,128)(2,1)} reshape(bf16[256,16384]{1,0:T(8,128)(2,1)} %convolution_convert_fusion.2) | data formatting | bytes 16777216 | tf_op jit(solution)/shard_map/while/body/eval_jaxpr/reshape | solution.py:91
  324.8 7.2 %fusion.44 = bf16[8,8,512,128]{3,2,1,0:T(8,128)(2,1)} fusion(bf16[8,8,512,128]{3,2,1,0:T(8,128)(2,1)} %get-tuple-element.145, s32[]{:T(128)} %get-tuple-element.144, bf16[8,1024,512]{2,1,0:T(8,128)(2,1)} %reshape.111, f32[8,512]{1,0:T(8,128)S(1)} %dynamic-slice_maximum_fusion.2, f32[128]{0:T(128)S(1)} %get-tuple-element.163, ...), kind=kOutput, calls=%fused_computation.3.clone.1 | convolution fusion | flops 1075314688 | bytes 9716736 | tf_op jit(solution)/shard_map/while/body/eval_jaxpr/dot_general | solution.py:94
  332.0 0.6 dynamic_slice.23
  333.2 9.0 %convolution_convert_fusion.2 = bf16[256,16384]{1,0:T(8,128)(2,1)} fusion(bf16[256,16384]{1,0:T(8,128)(2,1)} %get-tuple-element.161, bf16[256,2048]{0,1:T(8,128)(2,1)S(1)} %get-tuple-element.160, s32[]{:T(128)S(6)} %select_n.12), kind=kOutput, calls=%fused_computation.clone.1 | convolution fusion | flops 2151677952 | bytes 16908292 | tf_op jit(solution)/shard_map/while/body/eval_jaxpr/dot_general | solution.py:88
  342.2 13.6 %reshape.111 = bf16[8,1024,512]{2,1,0:T(8,128)(2,1)} reshape(bf16[256,16384]{1,0:T(8,128)(2,1)} %convolution_convert_fusion.2) | data formatting | bytes 16777216 | tf_op jit(solution)/shard_map/while/body/eval_jaxpr/reshape | solution.py:91
  357.7 7.2 %fusion.44 = bf16[8,8,512,128]{3,2,1,0:T(8,128)(2,1)} fusion(bf16[8,8,512,128]{3,2,1,0:T(8,128)(2,1)} %get-tuple-element.145, s32[]{:T(128)} %get-tuple-element.144, bf16[8,1024,512]{2,1,0:T(8,128)(2,1)} %reshape.111, f32[8,512]{1,0:T(8,128)S(1)} %dynamic-slice_maximum_fusion.2, f32[128]{0:T(128)S(1)} %get-tuple-element.163, ...), kind=kOutput, calls=%fused_computation.3.clone.1 | convolution fusion | flops 1075314688 | bytes 9716736 | tf_op jit(solution)/shard_map/while/body/eval_jaxpr/dot_general | solution.py:94
  364.9 0.6 dynamic_slice.23
  366.2 9.0 %convolution_convert_fusion.2 = bf16[256,16384]{1,0:T(8,128)(2,1)} fusion(bf16[256,16384]{1,0:T(8,128)(2,1)} %get-tuple-element.161, bf16[256,2048]{0,1:T(8,128)(2,1)S(1)} %get-tuple-element.160, s32[]{:T(128)S(6)} %select_n.12), kind=kOutput, calls=%fused_computation.clone.1 | convolution fusion | flops 2151677952 | bytes 16908292 | tf_op jit(solution)/shard_map/while/body/eval_jaxpr/dot_general | solution.py:88
  375.1 13.6 %reshape.111 = bf16[8,1024,512]{2,1,0:T(8,128)(2,1)} reshape(bf16[256,16384]{1,0:T(8,128)(2,1)} %convolution_convert_fusion.2) | data formatting | bytes 16777216 | tf_op jit(solution)/shard_map/while/body/eval_jaxpr/reshape | solution.py:91
  390.6 7.2 %fusion.44 = bf16[8,8,512,128]{3,2,1,0:T(8,128)(2,1)} fusion(bf16[8,8,512,128]{3,2,1,0:T(8,128)(2,1)} %get-tuple-element.145, s32[]{:T(128)} %get-tuple-element.144, bf16[8,1024,512]{2,1,0:T(8,128)(2,1)} %reshape.111, f32[8,512]{1,0:T(8,128)S(1)} %dynamic-slice_maximum_fusion.2, f32[128]{0:T(128)S(1)} %get-tuple-element.163, ...), kind=kOutput, calls=%fused_computation.3.clone.1 | convolution fusion | flops 1075314688 | bytes 9716736 | tf_op jit(solution)/shard_map/while/body/eval_jaxpr/dot_general | solution.py:94
  397.8 0.6 dynamic_slice.23
  399.1 9.0 %convolution_convert_fusion.2 = bf16[256,16384]{1,0:T(8,128)(2,1)} fusion(bf16[256,16384]{1,0:T(8,128)(2,1)} %get-tuple-element.161, bf16[256,2048]{0,1:T(8,128)(2,1)S(1)} %get-tuple-element.160, s32[]{:T(128)S(6)} %select_n.12), kind=kOutput, calls=%fused_computation.clone.1 | convolution fusion | flops 2151677952 | bytes 16908292 | tf_op jit(solution)/shard_map/while/body/eval_jaxpr/dot_general | solution.py:88
  408.0 13.6 %reshape.111 = bf16[8,1024,512]{2,1,0:T(8,128)(2,1)} reshape(bf16[256,16384]{1,0:T(8,128)(2,1)} %convolution_convert_fusion.2) | data formatting | bytes 16777216 | tf_op jit(solution)/shard_map/while/body/eval_jaxpr/reshape | solution.py:91
  423.6 7.2 %fusion.44 = bf16[8,8,512,128]{3,2,1,0:T(8,128)(2,1)} fusion(bf16[8,8,512,128]{3,2,1,0:T(8,128)(2,1)} %get-tuple-element.145, s32[]{:T(128)} %get-tuple-element.144, bf16[8,1024,512]{2,1,0:T(8,128)(2,1)} %reshape.111, f32[8,512]{1,0:T(8,128)S(1)} %dynamic-slice_maximum_fusion.2, f32[128]{0:T(128)S(1)} %get-tuple-element.163, ...), kind=kOutput, calls=%fused_computation.3.clone.1 | convolution fusion | flops 1075314688 | bytes 9716736 | tf_op jit(solution)/shard_map/while/body/eval_jaxpr/dot_general | solution.py:94
  430.7 0.6 dynamic_slice.23
  432.0 9.0 %convolution_convert_fusion.2 = bf16[256,16384]{1,0:T(8,128)(2,1)} fusion(bf16[256,16384]{1,0:T(8,128)(2,1)} %get-tuple-element.161, bf16[256,2048]{0,1:T(8,128)(2,1)S(1)} %get-tuple-element.160, s32[]{:T(128)S(6)} %select_n.12), kind=kOutput, calls=%fused_computation.clone.1 | convolution fusion | flops 2151677952 | bytes 16908292 | tf_op jit(solution)/shard_map/while/body/eval_jaxpr/dot_general | solution.py:88
  441.0 13.6 %reshape.111 = bf16[8,1024,512]{2,1,0:T(8,128)(2,1)} reshape(bf16[256,16384]{1,0:T(8,128)(2,1)} %convolution_convert_fusion.2) | data formatting | bytes 16777216 | tf_op jit(solution)/shard_map/while/body/eval_jaxpr/reshape | solution.py:91
  456.5 7.2 %fusion.44 = bf16[8,8,512,128]{3,2,1,0:T(8,128)(2,1)} fusion(bf16[8,8,512,128]{3,2,1,0:T(8,128)(2,1)} %get-tuple-element.145, s32[]{:T(128)} %get-tuple-element.144, bf16[8,1024,512]{2,1,0:T(8,128)(2,1)} %reshape.111, f32[8,512]{1,0:T(8,128)S(1)} %dynamic-slice_maximum_fusion.2, f32[128]{0:T(128)S(1)} %get-tuple-element.163, ...), kind=kOutput, calls=%fused_computation.3.clone.1 | convolution fusion | flops 1075314688 | bytes 9716736 | tf_op jit(solution)/shard_map/while/body/eval_jaxpr/dot_general | solution.py:94
  463.6 0.6 dynamic_slice.23
  464.9 9.0 %convolution_convert_fusion.2 = bf16[256,16384]{1,0:T(8,128)(2,1)} fusion(bf16[256,16384]{1,0:T(8,128)(2,1)} %get-tuple-element.161, bf16[256,2048]{0,1:T(8,128)(2,1)S(1)} %get-tuple-element.160, s32[]{:T(128)S(6)} %select_n.12), kind=kOutput, calls=%fused_computation.clone.1 | convolution fusion | flops 2151677952 | bytes 16908292 | tf_op jit(solution)/shard_map/while/body/eval_jaxpr/dot_general | solution.py:88
  473.9 13.6 %reshape.111 = bf16[8,1024,512]{2,1,0:T(8,128)(2,1)} reshape(bf16[256,16384]{1,0:T(8,128)(2,1)} %convolution_convert_fusion.2) | data formatting | bytes 16777216 | tf_op jit(solution)/shard_map/while/body/eval_jaxpr/reshape | solution.py:91
  489.4 7.2 %fusion.44 = bf16[8,8,512,128]{3,2,1,0:T(8,128)(2,1)} fusion(bf16[8,8,512,128]{3,2,1,0:T(8,128)(2,1)} %get-tuple-element.145, s32[]{:T(128)} %get-tuple-element.144, bf16[8,1024,512]{2,1,0:T(8,128)(2,1)} %reshape.111, f32[8,512]{1,0:T(8,128)S(1)} %dynamic-slice_maximum_fusion.2, f32[128]{0:T(128)S(1)} %get-tuple-element.163, ...), kind=kOutput, calls=%fused_computation.3.clone.1 | convolution fusion | flops 1075314688 | bytes 9716736 | tf_op jit(solution)/shard_map/while/body/eval_jaxpr/dot_general | solution.py:94
  496.5 0.6 dynamic_slice.23
  497.8 9.0 %convolution_convert_fusion.2 = bf16[256,16384]{1,0:T(8,128)(2,1)} fusion(bf16[256,16384]{1,0:T(8,128)(2,1)} %get-tuple-element.161, bf16[256,2048]{0,1:T(8,128)(2,1)S(1)} %get-tuple-element.160, s32[]{:T(128)S(6)} %select_n.12), kind=kOutput, calls=%fused_computation.clone.1 | convolution fusion | flops 2151677952 | bytes 16908292 | tf_op jit(solution)/shard_map/while/body/eval_jaxpr/dot_general | solution.py:88
  506.8 13.6 %reshape.111 = bf16[8,1024,512]{2,1,0:T(8,128)(2,1)} reshape(bf16[256,16384]{1,0:T(8,128)(2,1)} %convolution_convert_fusion.2) | data formatting | bytes 16777216 | tf_op jit(solution)/shard_map/while/body/eval_jaxpr/reshape | solution.py:91
  522.3 7.2 %fusion.44 = bf16[8,8,512,128]{3,2,1,0:T(8,128)(2,1)} fusion(bf16[8,8,512,128]{3,2,1,0:T(8,128)(2,1)} %get-tuple-element.145, s32[]{:T(128)} %get-tuple-element.144, bf16[8,1024,512]{2,1,0:T(8,128)(2,1)} %reshape.111, f32[8,512]{1,0:T(8,128)S(1)} %dynamic-slice_maximum_fusion.2, f32[128]{0:T(128)S(1)} %get-tuple-element.163, ...), kind=kOutput, calls=%fused_computation.3.clone.1 | convolution fusion | flops 1075314688 | bytes 9716736 | tf_op jit(solution)/shard_map/while/body/eval_jaxpr/dot_general | solution.py:94
  529.5 0.6 dynamic_slice.23
  530.7 9.0 %convolution_convert_fusion.2 = bf16[256,16384]{1,0:T(8,128)(2,1)} fusion(bf16[256,16384]{1,0:T(8,128)(2,1)} %get-tuple-element.161, bf16[256,2048]{0,1:T(8,128)(2,1)S(1)} %get-tuple-element.160, s32[]{:T(128)S(6)} %select_n.12), kind=kOutput, calls=%fused_computation.clone.1 | convolution fusion | flops 2151677952 | bytes 16908292 | tf_op jit(solution)/shard_map/while/body/eval_jaxpr/dot_general | solution.py:88
  539.7 13.6 %reshape.111 = bf16[8,1024,512]{2,1,0:T(8,128)(2,1)} reshape(bf16[256,16384]{1,0:T(8,128)(2,1)} %convolution_convert_fusion.2) | data formatting | bytes 16777216 | tf_op jit(solution)/shard_map/while/body/eval_jaxpr/reshape | solution.py:91
  555.2 7.2 %fusion.44 = bf16[8,8,512,128]{3,2,1,0:T(8,128)(2,1)} fusion(bf16[8,8,512,128]{3,2,1,0:T(8,128)(2,1)} %get-tuple-element.145, s32[]{:T(128)} %get-tuple-element.144, bf16[8,1024,512]{2,1,0:T(8,128)(2,1)} %reshape.111, f32[8,512]{1,0:T(8,128)S(1)} %dynamic-slice_maximum_fusion.2, f32[128]{0:T(128)S(1)} %get-tuple-element.163, ...), kind=kOutput, calls=%fused_computation.3.clone.1 | convolution fusion | flops 1075314688 | bytes 9716736 | tf_op jit(solution)/shard_map/while/body/eval_jaxpr/dot_general | solution.py:94
  562.4 0.7 copy-done.1
  (53 shorter events, 0.3 us)
Async XLA Ops:
  6.5 277.5 %copy-start = (bf16[256,32]{0,1:T(8,128)(2,1)S(1)}, bf16[256,32]{0,1:T(8,128)(2,1)}, u32[]{:S(2)}) copy-start(bf16[256,32]{0,1:T(8,128)(2,1)} %param.18) | copy-start | bytes 49156
  6.5 7.4 %copy-start.3 = (bf16[8,512,256]{2,1,0:T(8,128)(2,1)S(1)}, bf16[8,512,256]{2,1,0:T(8,128)(2,1)}, u32[]{:S(2)}) copy-start(bf16[8,512,256]{2,1,0:T(8,128)(2,1)} %param.13) | copy-start | bytes 6291460
  6.5 8.7 %copy-start.4 = (bf16[8,512]{1,0:T(8,128)(2,1)S(1)}, bf16[8,512]{1,0:T(8,128)(2,1)}, u32[]{:S(2)}) copy-start(bf16[8,512]{1,0:T(8,128)(2,1)} %param.14) | copy-start | bytes 24580
  6.5 8.7 %copy-start.6 = (f32[256]{0:T(256)S(1)}, f32[256]{0:T(256)}, u32[]{:S(2)}) copy-start(f32[256]{0:T(256)} %param.16) | copy-start | bytes 3076
  6.5 8.7 %copy-start.5 = (f32[256]{0:T(256)S(1)}, f32[256]{0:T(256)}, u32[]{:S(2)}) copy-start(f32[256]{0:T(256)} %param.17) | copy-start | bytes 3076
  6.5 8.7 %copy-start.9 = (bf16[256,32]{0,1:T(8,128)(2,1)S(1)}, bf16[256,32]{0,1:T(8,128)(2,1)}, u32[]{:S(2)}) copy-start(bf16[256,32]{0,1:T(8,128)(2,1)} %param.20) | copy-start | bytes 49156
  6.6 8.7 %copy-start.10 = (f32[32]{0:T(128)S(1)}, f32[32]{0:T(128)}, u32[]{:S(2)}) copy-start(f32[32]{0:T(128)} %param.21) | copy-start | bytes 388
  6.6 90.1 %all-gather.3.cloned.1.call-start = ((), (), s32[]{:S(2)}) async-start(), calls=%async_computation.2 | async-start | bytes 10485760 | tf_op jit(solution)/shard_map/all_gather | solution.py:64
  10.9 287.9 %all-gather.5.cloned.1.call-start = ((), (), s32[]{:S(2)}) async-start(), calls=%async_computation.3 | async-start | bytes 8650752 | tf_op jit(solution)/shard_map/all_gather | solution.py:59
  96.7 142.9 %all-to-all-start = ((bf16[8,32,16384]{2,0,1:T(8,128)(2,1)}), bf16[8,32,16384]{2,0,1:T(8,128)(2,1)}, u32[]{:S(2)}, u32[]{:S(2)}) async-start(bf16[8,32,16384]{2,0,1:T(8,128)(2,1)} %bitcast.60), calls=%async_computation | async-start | bytes 16777216 | tf_op jit(solution)/shard_map/all_to_all | solution.py:68
  274.5 10.7 %copy-start.2 = (f32[32,8,64,256]{3,2,1,0:T(8,128)S(1)}, f32[32,8,64,256]{3,2,1,0:T(8,128)}, u32[]{:S(2)}) copy-start(f32[32,8,64,256]{3,2,1,0:T(8,128)} %copy.25) | copy-start | bytes 50331652
  285.2 13.2 %copy-start.7 = (f32[32]{0:T(128)S(1)}, f32[32]{0:T(128)}, u32[]{:S(2)}) copy-start(f32[32]{0:T(128)} %param.19) | copy-start | bytes 388
  293.9 5.0 copy-start.11
  309.3 15.5 %copy-start.8 = (bf16[1024,128]{1,0:T(8,128)(2,1)S(1)}, bf16[1024,128]{1,0:T(8,128)(2,1)}, u32[]{:S(2)}) copy-start(bf16[1024,128]{1,0:T(8,128)(2,1)} %get-tuple-element.162) | copy-start | bytes 786436 | tf_op jit(solution)/shard_map/while
  342.2 15.5 %copy-start.8 = (bf16[1024,128]{1,0:T(8,128)(2,1)S(1)}, bf16[1024,128]{1,0:T(8,128)(2,1)}, u32[]{:S(2)}) copy-start(bf16[1024,128]{1,0:T(8,128)(2,1)} %get-tuple-element.162) | copy-start | bytes 786436 | tf_op jit(solution)/shard_map/while
  375.1 15.5 %copy-start.8 = (bf16[1024,128]{1,0:T(8,128)(2,1)S(1)}, bf16[1024,128]{1,0:T(8,128)(2,1)}, u32[]{:S(2)}) copy-start(bf16[1024,128]{1,0:T(8,128)(2,1)} %get-tuple-element.162) | copy-start | bytes 786436 | tf_op jit(solution)/shard_map/while
  408.0 15.5 %copy-start.8 = (bf16[1024,128]{1,0:T(8,128)(2,1)S(1)}, bf16[1024,128]{1,0:T(8,128)(2,1)}, u32[]{:S(2)}) copy-start(bf16[1024,128]{1,0:T(8,128)(2,1)} %get-tuple-element.162) | copy-start | bytes 786436 | tf_op jit(solution)/shard_map/while
  441.0 15.5 %copy-start.8 = (bf16[1024,128]{1,0:T(8,128)(2,1)S(1)}, bf16[1024,128]{1,0:T(8,128)(2,1)}, u32[]{:S(2)}) copy-start(bf16[1024,128]{1,0:T(8,128)(2,1)} %get-tuple-element.162) | copy-start | bytes 786436 | tf_op jit(solution)/shard_map/while
  473.9 15.5 %copy-start.8 = (bf16[1024,128]{1,0:T(8,128)(2,1)S(1)}, bf16[1024,128]{1,0:T(8,128)(2,1)}, u32[]{:S(2)}) copy-start(bf16[1024,128]{1,0:T(8,128)(2,1)} %get-tuple-element.162) | copy-start | bytes 786436 | tf_op jit(solution)/shard_map/while
  506.8 15.5 %copy-start.8 = (bf16[1024,128]{1,0:T(8,128)(2,1)S(1)}, bf16[1024,128]{1,0:T(8,128)(2,1)}, u32[]{:S(2)}) copy-start(bf16[1024,128]{1,0:T(8,128)(2,1)} %get-tuple-element.162) | copy-start | bytes 786436 | tf_op jit(solution)/shard_map/while
  539.7 15.5 %copy-start.8 = (bf16[1024,128]{1,0:T(8,128)(2,1)S(1)}, bf16[1024,128]{1,0:T(8,128)(2,1)}, u32[]{:S(2)}) copy-start(bf16[1024,128]{1,0:T(8,128)(2,1)} %get-tuple-element.162) | copy-start | bytes 786436 | tf_op jit(solution)/shard_map/while
  562.4 0.7 copy-start.1
Sparse Core Ops, SparseCore 0:
  11.0 85.6 all-gather.2
  98.9 123.8 all-gather.4
where the time goes:
time: 576 us; the launch traced here: 570 us
  blocking collectives  163 us (28%)
  local copies, waits for them, and re-layouts  141 us (24%)
  matrix products  140 us (24%)
  waiting for transfers between devices  50.8 us (9%)
  other arithmetic  33.5 us (6%)
  loops' own time  20.6 us (4%)
  between operations  13.7 us (2%)
  starting transfers between devices  7.44 us (1%)
    all_gather x1, blocking collectives, per_device(): lax.all_gather(kept_mask, 'dap', axis=0, tiled=True)  135 us
    reshape x8, local copies, waits for them, and re-layouts, one_block(): outer.astype(jnp.bfloat16)  109 us
    dot_general x8, matrix products, one_block(): lax.dot_general(left_block, right_all, (((0,), (0,)), ((), ())), preferre...  71.9 us
    dot_general x8, matrix products, one_block(): lax.dot_general(outer, final_projection_matrix, (((1,), (0,)), ((), ())),...  57.3 us
    all_gather x1, waiting for transfers between devices, per_device(): lax.all_gather(raw_flat, 'rep', axis=1, tiled=True)  50.7 us
    unnamed x27, local copies, waits for them, and re-layouts  23 us
    another operation x1, loops' own time, per_device(): blocks = lax.map(one_block, offsets)  20.6 us
    all_to_all x1, blocking collectives, per_device(): lax.all_to_all(kept_wide, 'dap', split_axis=1, concat_axis=0, tiled=True)  15.4 us
  transfers between devices with their start and end apart: 3, of which 1 were waited for; matrix products, arithmetic and copies ran while one was open for 11% of the time, Pallas kernels for 0%

commit v1 on v0

v1 whole, which is shorter than its diff:
```python
import functools

import jax
import jax.numpy as jnp
from jax import lax
from jax.experimental import pallas as pl
from jax.experimental.pallas import tpu as pltpu
from jax.sharding import Mesh, PartitionSpec as P

F32 = jnp.float32
BF16 = jnp.bfloat16
ZN, XN, CN, YN = 4, 4, 2, 4
SEQ = 8
CHAN = 256
FEAT = 32
COLS = 512
CB = 128
NB = COLS // CB
ROWS = 64
RW = (FEAT + 1) * CB
LW = (FEAT + 2) * ROWS
OUT = 128
MIB = 2**20


def prepare_kernel(rep_ref, x_ref, pres_ref, gen_ref, sc_ref, of_ref, w_ref, b_ref, r_ref, l_ref, scr):
    kept = (pres_ref[...].astype(F32) * gen_ref[...].astype(F32)).astype(BF16).astype(F32)
    scale = sc_ref[...]
    offset = of_ref[...]
    w = w_ref[...]
    bias = b_ref[...]
    for s in range(SEQ):
        v = x_ref[s].astype(F32)
        centred = v - jnp.mean(v, axis=-1, keepdims=True)
        var = jnp.mean(centred * centred, axis=-1, keepdims=True)
        normed = (centred * lax.rsqrt(var + 1e-05) * scale + offset).astype(BF16)
        p = lax.dot_general(w, normed, (((1,), (1,)), ((), ())), preferred_element_type=F32)
        scr[s * 64 : (s + 1) * 64, :] = (p + bias) * kept[s : s + 1, :]
    for e in range(FEAT):
        r_ref[0, :, e * CB : (e + 1) * CB] = scr[pl.ds(FEAT + e, SEQ, stride=64), :].astype(BF16)
    r_ref[0, :, FEAT * CB :] = kept.astype(BF16)
    for pair in range(FEAT // 2 + 1):
        if pair < FEAT // 2:
            a = scr[pl.ds(2 * pair, SEQ, stride=64), :]
            b = scr[pl.ds(2 * pair + 1, SEQ, stride=64), :]
        else:
            a = kept
            b = jnp.zeros_like(kept)
        for d in range(2):
            both = jnp.concatenate([a[:, d * 64 : (d + 1) * 64], b[:, d * 64 : (d + 1) * 64]], axis=1)
            l_ref[d, :, pair * 128 : (pair + 1) * 128] = both.astype(BF16)


def prepare(rep, x, pres, gen, scale, offset, w, bias):
    return pl.pallas_call(
        prepare_kernel,
        grid_spec=pltpu.PrefetchScalarGridSpec(
            num_scalar_prefetch=1,
            grid=(NB,),
            in_specs=[
                pl.BlockSpec((SEQ, CB, CHAN), lambda q, rep: (0, q, 0)),
                pl.BlockSpec((SEQ, CB), lambda q, rep: (0, q)),
                pl.BlockSpec((1, CB), lambda q, rep: (0, rep[0] * NB + q)),
                pl.BlockSpec((1, CHAN), lambda q, rep: (0, 0)),
                pl.BlockSpec((1, CHAN), lambda q, rep: (0, 0)),
                pl.BlockSpec((2 * FEAT, CHAN), lambda q, rep: (0, 0)),
                pl.BlockSpec((2 * FEAT, 1), lambda q, rep: (0, 0)),
            ],
            out_specs=[
                pl.BlockSpec((1, SEQ, RW), lambda q, rep: (q, 0, 0)),
                pl.BlockSpec((2, SEQ, LW), lambda q, rep: (q, 0, 0)),
            ],
            scratch_shapes=[pltpu.VMEM((SEQ * 64, CB), F32)],
        ),
        out_shape=[
            jax.ShapeDtypeStruct((NB, SEQ, RW), BF16),
            jax.ShapeDtypeStruct((2 * NB, SEQ, LW), BF16),
        ],
        compiler_params=pltpu.CompilerParams(vmem_limit_bytes=32 * MIB),
        cost_estimate=pl.CostEstimate(flops=140_000_000, bytes_accessed=3 * MIB, transcendentals=4096),
        name="prepare",
    )(rep, x, pres, gen, scale, offset, w, bias)


def left_kernel(l_ref, lt_ref, kl_ref, scr):
    for h in range(2):
        half = slice(h * 128, (h + 1) * 128)
        scr[...] = l_ref[half, :].astype(F32).T
        for i in range(ROWS):
            lt_ref[i * FEAT : (i + 1) * FEAT, half] = scr[pl.ds(i, FEAT, stride=ROWS), :].astype(BF16)
        kl_ref[:, half] = scr[FEAT * ROWS : (FEAT + 1) * ROWS, :].astype(BF16)


def arrange_left(l):
    return pl.pallas_call(
        left_kernel,
        out_shape=[
            jax.ShapeDtypeStruct((ROWS * FEAT, 256), BF16),
            jax.ShapeDtypeStruct((ROWS, 256), BF16),
        ],
        scratch_shapes=[pltpu.VMEM((LW, 128), F32)],
        compiler_params=pltpu.CompilerParams(vmem_limit_bytes=32 * MIB),
        cost_estimate=pl.CostEstimate(flops=1_000_000, bytes_accessed=2 * MIB, transcendentals=0),
        name="arrange_left",
    )(l)


def pair_kernel(ib, first, q_ref, lt_ref, kl_ref, r_ref, w_ref, b_ref, *rest):
    o_ref, scr, rcp = rest[-3:]
    step = pl.program_id(0)

    @pl.when(step == 0)
    def _():
        counts = jnp.dot(kl_ref[...], r_ref[:, FEAT * CB :], preferred_element_type=F32)
        rcp[...] = 1.0 / jnp.maximum(counts, 1.0)

    o = jnp.dot(lt_ref[...], r_ref[:, : FEAT * CB], preferred_element_type=F32).astype(BF16)
    for i in range(ib):
        for e in range(FEAT):
            scr[e * FEAT : (e + 1) * FEAT, i * CB : (i + 1) * CB] = o[i * FEAT : (i + 1) * FEAT, e * CB : (e + 1) * CB]
    p = jnp.dot(w_ref[...], scr[...], preferred_element_type=F32)
    for i in range(ib):
        scale = rcp[pl.ds(step * ib + i, 1), :]
        o_ref[i] = ((p[:, i * CB : (i + 1) * CB] + b_ref[...]) * scale).T.astype(BF16)


def pair_block(q, lt, kl, r, w, bias, out, ib=16):
    specs = [
        pl.BlockSpec((ib * FEAT, 256), lambda i, q: (i, 0)),
        pl.BlockSpec((ROWS, 256), lambda i, q: (0, 0)),
        pl.BlockSpec((256, RW), lambda i, q: (0, 0)),
        pl.BlockSpec((OUT, FEAT * FEAT), lambda i, q: (0, 0)),
        pl.BlockSpec((OUT, 1), lambda i, q: (0, 0)),
    ]
    args = [q, lt, kl, r, w, bias]
    aliases = {}
    if out is not None:
        specs.append(pl.BlockSpec(memory_space=pl.ANY))
        args.append(out)
        aliases = {6: 0}
    return pl.pallas_call(
        functools.partial(pair_kernel, ib, out is None),
        grid_spec=pltpu.PrefetchScalarGridSpec(
            num_scalar_prefetch=1,
            grid=(ROWS // ib,),
            in_specs=specs,
            out_specs=pl.BlockSpec((ib, CB, OUT), lambda i, q: (i, q[0], 0)),
            scratch_shapes=[
                pltpu.VMEM((FEAT * FEAT, ib * CB), BF16),
                pltpu.VMEM((ROWS, CB), F32),
            ],
        ),
        out_shape=jax.ShapeDtypeStruct((ROWS, COLS, OUT), BF16),
        input_output_aliases=aliases,
        compiler_params=pltpu.CompilerParams(vmem_limit_bytes=48 * MIB),
        cost_estimate=pl.CostEstimate(
            flops=2 * ROWS * CB * FEAT * FEAT * (256 + OUT), bytes_accessed=6 * MIB, transcendentals=0
        ),
        name="pair_block",
    )(*args)


def shift(v, axis, by):
    return lax.ppermute(v, axis, [(i, (i + by) % 4) for i in range(4)])


def gather_chips(v):
    return lax.all_gather(v, ("z", "x"), axis=0, tiled=True)


def per_device(x, pres, gen, scale, offset, w1, b1, w2, b2, wf, bf):
    core = lax.axis_index("core")
    rep = lax.axis_index("rep").astype(jnp.int32).reshape(1)
    w = jnp.concatenate([w1, w2], axis=1).T
    bias = jnp.concatenate([b1, b2]).reshape(2 * FEAT, 1)
    wt = jnp.transpose(wf.reshape(FEAT, FEAT, OUT), (2, 1, 0)).reshape(OUT, FEAT * FEAT)
    r, l = prepare(
        rep, x, pres, gen.reshape(1, -1), scale.reshape(1, -1), offset.reshape(1, -1), w, bias
    )
    l = lax.ppermute(l, ("z", "rep"), [(z * 4 + y, y * 4 + z) for z in range(4) for y in range(4)])
    l = lax.all_to_all(l, ("x", "core"), split_axis=0, concat_axis=0, tiled=True)
    l = lax.all_gather(l.reshape(XN * CN * SEQ, LW), "rep", axis=0, tiled=True)
    lt, kl = arrange_left(l)
    r = r.reshape(CN, 2, SEQ, RW)
    r = lax.all_to_all(r, "core", split_axis=0, concat_axis=2, tiled=True).reshape(2, CN * SEQ, RW)
    own = [gather_chips(r[k]) for k in range(2)]
    other = [lax.ppermute(v, "core", [(0, 1), (1, 0)]) for v in own]
    out = None
    bf = bf.reshape(OUT, 1)
    for c, rs in ((core, own), (1 - core, other)):
        for k in range(2):
            q = (c * 2 + k).astype(jnp.int32).reshape(1)
            out = pair_block(q, lt, kl, rs[k], wt, bf, out)
    return out


def solution(mesh):
    grid = Mesh(mesh.devices.reshape(ZN, XN, CN, YN), ("z", "x", "core", "rep"))
    dap = ("z", "x", "core")
    in_specs = (P(dap, "rep", None), P(dap, "rep"), P(), P(), P(), P(), P(), P(), P(), P(), P())
    return jax.shard_map(
        per_device, mesh=grid, in_specs=in_specs, out_specs=P(dap, "rep", None), check_vma=False
    )
```

time: 576 us -> 196 us (0.34); the launches traced: 570 us -> 196 us
  blocking collectives: 163 us -> 15.9 us
  matrix products: 140 us -> 0 us
  local copies, waits for them, and re-layouts: 141 us -> 8.4 us
  waiting for transfers between devices: 50.8 us -> 111 us
  Pallas kernels: 0 us -> 45.1 us
  other arithmetic: 33.5 us -> 1.48 us
  loops' own time: 20.6 us -> 0 us
  starting transfers between devices: 7.44 us -> 0.76 us
    all_gather x2 -> x0, blocking collectives: 148 us -> none  [the longest x1 135 us: per_device(): lax.all_gather(kept_mask, 'dap', axis=0, tiled=True)]
    dot_general x19 -> x0, matrix products: 140 us -> none  [the longest x8 71.9 us: one_block(): lax.dot_general(left_block, right_all, (((0,), (0,)), ((), ())), preferre...]
    reshape x8 -> x3, local copies, waits for them, and re-layouts: 109 us -> 0.36 us  [the longest x1 0.14 us: per_device(): jnp.transpose(wf.reshape(FEAT, FEAT, OUT), (2, 1, 0))]
    all_gather x2 -> x3, waiting for transfers between devices: 50.8 us -> 110 us  [the longest x2 85.5 us: gather_chips(): return lax.all_gather(v, ('z', 'x'), axis=0, tiled=True)]
    pallas_call x0 -> x6, Pallas kernels: none -> 45.1 us  [the longest x4 40.3 us: pair_block(): pl.pallas_call(functools.partial(pair_kernel, ib, out is None), grid_spec...]
    reduce_sum x4 -> x0, other arithmetic: 21 us -> none  [the longest x2 10.8 us: standardize_features(): variance = jnp.mean(centred * centred, axis=-1, keepdims=True)]
    another operation x1 -> x0, loops' own time: 20.6 us -> none  [per_device(): blocks = lax.map(one_block, offsets)]
    unnamed x27 -> x20, local copies, waits for them, and re-layouts: 23 us -> 7.2 us
  transfers between devices with their start and end apart: 3 -> 6, of which waited for: 1 -> 3; matrix products, arithmetic and copies ran while one was open for 11% -> 0% of each run, Pallas kernels for 0% -> 16%
where the time goes in v1:
time: 196 us
  waiting for transfers between devices  111 us (57%)
  Pallas kernels  45.1 us (23%)
  blocking collectives  15.9 us (8%)
  between operations  13.2 us (7%)
  local copies, waits for them, and re-layouts  8.4 us (4%)
    all_gather x2, waiting for transfers between devices, gather_chips(): return lax.all_gather(v, ('z', 'x'), axis=0, tiled=True)  85.5 us
    pallas_call x4, Pallas kernels, pair_block(): pl.pallas_call(functools.partial(pair_kernel, ib, out is None), grid_spec...  40.3 us
    all_gather x1, waiting for transfers between devices, per_device(): l = lax.all_gather(l.reshape(XN * CN * SEQ, LW), 'rep', axis=0, tiled=True)  24.8 us
    all_to_all x1, blocking collectives, per_device(): lax.all_to_all(l, ('x', 'core'), split_axis=0, concat_axis=0, tiled=True)  12 us
    unnamed x20, local copies, waits for them, and re-layouts  7.2 us
  transfers between devices with their start and end apart: 6, of which 3 were waited for; matrix products, arithmetic and copies ran while one was open for 0% of the time, Pallas kernels for 16%

profile of v1, /device:TPU:0, one launch (start us, length us, event | category | flops | bytes accessed | tf_op | source)
XLA Modules:
  0.0 195.9 jit_solution(15453992584062586851)
XLA Ops:
  6.5 0.0 all-gather.8.cloned.1.call-start
  6.5 0.7 maximum_bitcast_fusion.1
  7.3 0.1 copy.43.b_ref
  7.4 0.7 maximum_bitcast_fusion.w_ref
  8.1 0.0 copy-start
  8.1 1.6 copy-done
  9.7 0.0 copy-start.2
  9.7 0.7 copy-done.2
  10.4 0.0 copy-start.3
  10.4 0.7 copy-done.3
  11.1 0.0 copy-start.4
  11.1 0.7 copy-done.4
  11.8 0.0 copy-start.5
  11.8 0.7 copy-done.5
  12.5 0.0 copy-start.8
  12.5 3.3 %prepare.1 = (bf16[4,8,4224]{2,1,0:T(8,128)(2,1)S(1)}, bf16[8,8,2176]{2,1,0:T(8,128)(2,1)S(1)}) custom-call(s32[1]{0:T(128)} %bitcast.1.rep_ref, bf16[8,512,256]{2,1,0:T(8,128)(2,1)S(1)} %copy-done, bf16[8,512]{1,0:T(8,128)(2,1)S(1)} %copy-done.2, s32[1,2048]{1,0:T(1,128)S(1)} %bitcast.27, f32[1,256]{1,0:T(1,128)S(1)} %bitcast.28, f32[1,256]{1,0:T(1,128)S(1)} %bitcast.29, ...), custom_call_target="tpu_custom_call" | custom-call | flops 140000000 | bytes 3145728 | tf_op jit(solution)/shard_map/prepare/pallas_call | solution.py:55
  15.8 0.0 copy-start.9
  15.8 3.9 %all_to_all.20 = bf16[2,2,8,4224]{3,2,1,0:T(8,128)(2,1)S(1)} all-to-all(bf16[2,2,8,4224]{3,2,1,0:T(8,128)(2,1)S(1)} %bitcast.26), channel_id=1, replica_groups=mesh['z'=4,'x'=4,'core'=2,'rep'=4] {'core'}, dimensions={0} | all-to-all | bytes 540672 | tf_op jit(solution)/shard_map/all_to_all | solution.py:185
  19.7 0.7 slice_bitcast_fusion
  20.5 0.0 all-gather.8.cloned.1.call-update
  20.5 0.0 all-gather.6.cloned.1.call-start
  20.6 0.7 all-gather.6.cloned.1.call-update
  21.3 0.0 all-gather.4.cloned.1.call-start
  21.3 0.7 collective-permute-start
  22.0 0.0 collective-permute-done
  22.0 12.0 %all_to_all.21 = bf16[8,8,2176]{2,1,0:T(8,128)(2,1)} all-to-all(bf16[8,8,2176]{2,1,0:T(8,128)(2,1)S(1)} %collective-permute-done), channel_id=1, replica_groups=mesh['z'=4,'x'=4,'core'=2,'rep'=4] {'x','core'}, dimensions={0} | all-to-all | bytes 557056 | tf_op jit(solution)/shard_map/all_to_all | solution.py:181
  34.0 0.0 all-gather.4.cloned.1.call-update
  34.0 38.7 %all-gather.8.cloned.1.call-done.r_ref = bf16[256,4224]{1,0:T(8,128)(2,1)} async-done(((bf16[16,4224]{1,0:T(8,128)(2,1)}), bf16[256,4224]{1,0:T(8,128)(2,1)}) %all-gather.8.cloned.1.call-update) | async-done | bytes 2162704 | tf_op jit(solution)/shard_map/all_gather | solution.py:168
  72.7 0.0 collective-permute-start.2
  72.7 46.8 %all-gather.6.cloned.1.call-done.r_ref = bf16[256,4224]{1,0:T(8,128)(2,1)} async-done(((bf16[16,4224]{1,0:T(8,128)(2,1)}), bf16[256,4224]{1,0:T(8,128)(2,1)}) %all-gather.6.cloned.1.call-update) | async-done | bytes 2162704 | tf_op jit(solution)/shard_map/all_gather | solution.py:168
  119.5 0.0 collective-permute-start.1
  119.5 0.0 copy-done.8
  119.5 0.1 copy.44
  119.6 0.1 copy.51.w_ref
  119.8 0.0 copy-done.9
  119.8 0.1 copy.52.b_ref
  119.9 24.8 %all-gather.4.cloned.1.call-done.l_ref = bf16[256,2176]{1,0:T(8,128)(2,1)} async-done(((bf16[64,2176]{1,0:T(8,128)(2,1)}), bf16[256,2176]{1,0:T(8,128)(2,1)}) %all-gather.4.cloned.1.call-update) | async-done | bytes 1114128 | tf_op jit(solution)/shard_map/all_gather | solution.py:182
  144.7 0.0 copy-start.1
  144.7 1.2 copy-done.1
  145.9 1.4 arrange_left.1
  147.4 0.0 copy-start.6
  147.4 1.6 copy-done.6
  149.0 0.0 copy-start.7
  149.0 9.7 %pair_block.4.rest_0_ = bf16[64,512,128]{2,1,0:T(8,128)(2,1)} custom-call(s32[1]{0:T(128)} %bitcast.20.q_ref, bf16[2048,256]{1,0:T(8,128)(2,1)S(1)} %get-tuple-element.10.lt_ref, bf16[64,256]{1,0:T(8,128)(2,1)S(1)} %get-tuple-element.11.kl_ref, bf16[256,4224]{1,0:T(8,128)(2,1)S(1)} %copy-done.6, bf16[128,1024]{1,0:T(8,128)(2,1)S(1)} %copy.51.w_ref, ...), custom_call_target="tpu_custom_call" | custom-call | flops 6442450944 | bytes 6291456 | tf_op jit(solution)/shard_map/pair_block/pallas_call | solution.py:141
  158.7 0.0 copy-done.7
  158.7 9.7 %pair_block.5.rest_0_ = bf16[64,512,128]{2,1,0:T(8,128)(2,1)} custom-call(s32[1]{0:T(128)} %bitcast.19.q_ref, bf16[2048,256]{1,0:T(8,128)(2,1)S(1)} %get-tuple-element.10.lt_ref, bf16[64,256]{1,0:T(8,128)(2,1)S(1)} %get-tuple-element.11.kl_ref, bf16[256,4224]{1,0:T(8,128)(2,1)S(1)} %copy-done.7, ...), custom_call_target="tpu_custom_call", output_to_operand_aliasing={{}: (6, {})} | custom-call | flops 6442450944 | bytes 6291456 | tf_op jit(solution)/shard_map/pair_block/pallas_call | solution.py:141
  168.3 0.0 collective-permute-done.2.r_ref
  168.3 9.7 %pair_block.6.rest_0_ = bf16[64,512,128]{2,1,0:T(8,128)(2,1)} custom-call(s32[1]{0:T(128)} %bitcast.16.q_ref, bf16[2048,256]{1,0:T(8,128)(2,1)S(1)} %get-tuple-element.10.lt_ref, bf16[64,256]{1,0:T(8,128)(2,1)S(1)} %get-tuple-element.11.kl_ref, bf16[256,4224]{1,0:T(8,128)(2,1)S(1)} %collective-permute-done.2.r_ref, ...), custom_call_target="tpu_custom_call", output_to_operand_aliasing={{}: (6, {})} | custom-call | flops 6442450944 | bytes 6291456 | tf_op jit(solution)/shard_map/pair_block/pallas_call | solution.py:141
  178.0 0.0 collective-permute-done.1.r_ref
  178.0 11.3 %pair_block.7 = bf16[64,512,128]{2,1,0:T(8,128)(2,1)} custom-call(s32[1]{0:T(128)} %bitcast.q_ref, bf16[2048,256]{1,0:T(8,128)(2,1)S(1)} %get-tuple-element.10.lt_ref, bf16[64,256]{1,0:T(8,128)(2,1)S(1)} %get-tuple-element.11.kl_ref, bf16[256,4224]{1,0:T(8,128)(2,1)} %collective-permute-done.1.r_ref, ...), custom_call_target="tpu_custom_call", output_to_operand_aliasing={{}: (6, {})} | custom-call | flops 6442450944 | bytes 6291456 | tf_op jit(solution)/shard_map/pair_block/pallas_call | solution.py:141
Async XLA Ops:
  6.5 66.2 %all-gather.8.cloned.1.call-start = ((), (), s32[]{:S(2)}) async-start(), calls=%async_computation.4 | async-start | bytes 2297856 | tf_op jit(solution)/shard_map/all_gather | solution.py:168
  8.1 1.6 copy-start
  9.7 0.7 copy-start.2
  10.4 0.7 copy-start.3
  11.1 0.7 copy-start.4
  11.8 0.7 copy-start.5
  12.5 107.0 %copy-start.8 = (bf16[1024,128]{1,0:T(8,128)(2,1)S(1)}, bf16[1024,128]{1,0:T(8,128)(2,1)}, u32[]{:S(2)}) copy-start(bf16[1024,128]{1,0:T(8,128)(2,1)} %param.20) | copy-start | bytes 786436
  15.8 104.0 %copy-start.9 = (f32[128]{0:T(128)S(1)}, f32[128]{0:T(128)}, u32[]{:S(2)}) copy-start(f32[128]{0:T(128)} %param.21) | copy-start | bytes 1540
  20.5 99.0 %all-gather.6.cloned.1.call-start = ((), (), s32[]{:S(2)}) async-start(), calls=%async_computation.3 | async-start | bytes 2297856 | tf_op jit(solution)/shard_map/all_gather | solution.py:168
  21.3 123.4 %all-gather.4.cloned.1.call-start = ((), (), s32[]{:S(2)}) async-start(), calls=%async_computation.2 | async-start | bytes 1392640 | tf_op jit(solution)/shard_map/all_gather | solution.py:182
  21.3 0.7 collective-permute-start
  72.7 95.6 %collective-permute-start.2 = (bf16[256,4224]{1,0:T(8,128)(2,1)}, bf16[256,4224]{1,0:T(8,128)(2,1)S(1)}, u32[]{:S(2)}, u32[]{:S(2)}) collective-permute-start(bf16[256,4224]{1,0:T(8,128)(2,1)} %all-gather.8.cloned.1.call-done.r_ref), channel_id=1, source_target_pairs={{0,4},{4,0},{1,5},{5,1},{2,6},{6,2},{3,7},{7,3},{8,12},{12,8},{9,1... | collective-permute-start | bytes 6488072 | tf_op jit(solution)/shard_map/ppermute | solution.py:187
  119.5 58.5 %collective-permute-start.1 = (bf16[256,4224]{1,0:T(8,128)(2,1)}, bf16[256,4224]{1,0:T(8,128)(2,1)}, u32[]{:S(2)}, u32[]{:S(2)}) collective-permute-start(bf16[256,4224]{1,0:T(8,128)(2,1)} %all-gather.6.cloned.1.call-done.r_ref), channel_id=1, source_target_pairs={{0,4},{4,0},{1,5},{5,1},{2,6},{6,2},{3,7},{7,3},{8,12},{12,8},{9,1... | collective-permute-start | bytes 6488072 | tf_op jit(solution)/shard_map/ppermute | solution.py:187
  144.7 1.2 copy-start.1
  147.4 1.6 copy-start.6
  149.0 9.7 %copy-start.7 = (bf16[256,4224]{1,0:T(8,128)(2,1)S(1)}, bf16[256,4224]{1,0:T(8,128)(2,1)}, u32[]{:S(2)}) copy-start(bf16[256,4224]{1,0:T(8,128)(2,1)} %all-gather.6.cloned.1.call-done.r_ref) | copy-start | bytes 6488068
Sparse Core Ops, SparseCore 0:
  20.6 52.0 all-gather.7
  74.9 44.5 all-gather.5
  121.2 23.4 all-gather.3

commit v2 on v1

v2 whole, which is shorter than its diff:
```python
import functools

import jax
import jax.numpy as jnp
from jax import lax
from jax.experimental import pallas as pl
from jax.experimental.pallas import tpu as pltpu
from jax.sharding import Mesh, PartitionSpec as P

F32 = jnp.float32
BF16 = jnp.bfloat16
ZN, XN, CN, YN = 4, 4, 2, 4
SEQ = 8
CHAN = 256
FEAT = 32
COLS = 512
CB = 128
NB = COLS // CB
ROWS = 64
HALF = FEAT // 2
RW = (HALF + 1) * CB
LW = (FEAT + 2) * ROWS
SW = 4 * RW + XN * LW
OUT = 128
RING = (0, -1, 1, 2)
MIB = 2**20


def prepare_kernel(
    rep_ref, x_ref, pres_ref, gen_ref, sc_ref, of_ref, w1_ref, b1_ref, w2_ref, b2_ref, keep_ref, send_ref, scr, w_scr, b_scr
):
    q = pl.program_id(0)

    @pl.when(q == 0)
    def _():
        w_scr[:FEAT, :] = w1_ref[...]
        w_scr[FEAT:, :] = w2_ref[...]
        b_scr[:FEAT, :] = jnp.broadcast_to(b1_ref[...], (CB, FEAT)).T
        b_scr[FEAT:, :] = jnp.broadcast_to(b2_ref[...], (CB, FEAT)).T

    kept = (pres_ref[...].astype(F32) * gen_ref[...].astype(F32)).astype(BF16).astype(F32)
    scale = sc_ref[...]
    offset = of_ref[...]
    w = w_scr[...]
    bias = b_scr[...]
    for s in range(SEQ):
        v = x_ref[s].astype(F32)
        centred = v - jnp.mean(v, axis=-1, keepdims=True)
        var = jnp.mean(centred * centred, axis=-1, keepdims=True)
        normed = (centred * lax.rsqrt(var + 1e-05) * scale + offset).astype(BF16)
        p = lax.dot_general(w, normed, (((1,), (1,)), ((), ())), preferred_element_type=F32)
        scr[s * 64 : (s + 1) * 64, :] = (p + bias) * kept[s : s + 1, :]
    core = lax.axis_index("core")

    def put_right(ref):
        for half in range(2):
            base = (half * 2 + lax.rem(q, 2)) * RW
            for e in range(HALF + 1):
                v = scr[pl.ds(FEAT + half * HALF + e, SEQ, stride=64), :] if e < HALF else kept
                ref[:, pl.ds(pl.multiple_of(base + e * CB, CB), CB)] = v.astype(BF16)

    pl.when(q // 2 == core)(lambda: put_right(keep_ref))
    pl.when(q // 2 != core)(lambda: put_right(send_ref))

    def put_left(refs):
        for pair in range(FEAT // 2 + 1):
            if pair < FEAT // 2:
                a = scr[pl.ds(2 * pair, SEQ, stride=64), :]
                b = scr[pl.ds(2 * pair + 1, SEQ, stride=64), :]
            else:
                a = kept
                b = jnp.zeros_like(kept)
            for d, ref in enumerate(refs):
                both = jnp.concatenate([a[:, d * 64 : (d + 1) * 64], b[:, d * 64 : (d + 1) * 64]], axis=1)
                at = pl.multiple_of(4 * RW + q * LW + pair * 128, 128)
                ref[:, pl.ds(at, 128)] = both.astype(BF16)

    pl.when(core == 0)(lambda: put_left((keep_ref, send_ref)))
    pl.when(core == 1)(lambda: put_left((send_ref, keep_ref)))


def prepare(rep, x, pres, gen, scale, offset, w1, b1, w2, b2):
    whole = lambda *shape: pl.BlockSpec(shape, lambda q, rep: (0, 0))
    return pl.pallas_call(
        prepare_kernel,
        grid_spec=pltpu.PrefetchScalarGridSpec(
            num_scalar_prefetch=1,
            grid=(NB,),
            in_specs=[
                pl.BlockSpec((SEQ, CB, CHAN), lambda q, rep: (0, q, 0)),
                pl.BlockSpec((SEQ, CB), lambda q, rep: (0, q)),
                pl.BlockSpec((1, CB), lambda q, rep: (0, rep[0] * NB + q)),
                whole(1, CHAN),
                whole(1, CHAN),
                whole(FEAT, CHAN),
                whole(1, FEAT),
                whole(FEAT, CHAN),
                whole(1, FEAT),
            ],
            out_specs=[pl.BlockSpec((SEQ, SW), lambda q, rep: (0, 0))] * 2,
            scratch_shapes=[
                pltpu.VMEM((SEQ * 64, CB), F32),
                pltpu.VMEM((2 * FEAT, CHAN), BF16),
                pltpu.VMEM((2 * FEAT, CB), F32),
            ],
        ),
        out_shape=[jax.ShapeDtypeStruct((SEQ, SW), BF16)] * 2,
        compiler_params=pltpu.CompilerParams(vmem_limit_bytes=60 * MIB),
        cost_estimate=pl.CostEstimate(flops=140_000_000, bytes_accessed=3 * MIB, transcendentals=4096),
        name="prepare",
    )(rep, x, pres, gen, scale, offset, w1, b1, w2, b2)


def split_kernel(keep_ref, got_ref, l_ref, first_ref, second_ref, *x_refs):
    core, x = lax.axis_index("core"), lax.axis_index("x")

    def both(lanes):
        keep, got = keep_ref[:, lanes].astype(F32), got_ref[:, lanes].astype(F32)
        rows = [jnp.where(core == 0, keep, got), jnp.where(core == 0, got, keep)]
        return jnp.concatenate(rows, axis=0).astype(BF16)

    first = both(slice(0, 2 * RW))
    first_ref[...] = first
    second_ref[...] = both(slice(2 * RW, 4 * RW))
    for away, ref in zip(RING, (l_ref,) + x_refs):
        left = both(pl.ds(pl.multiple_of(4 * RW + lax.rem(x - away + 4, 4) * LW, 128), LW))
        if away == 0:
            ref[...] = left
        else:
            ref[:, : 2 * RW] = first
            ref[:, 2 * RW :] = left


def split(keep, got):
    return pl.pallas_call(
        split_kernel,
        out_shape=[jax.ShapeDtypeStruct((16, n), BF16) for n in (LW, 2 * RW, 2 * RW) + (2 * RW + LW,) * 3],
        compiler_params=pltpu.CompilerParams(vmem_limit_bytes=16 * MIB),
        cost_estimate=pl.CostEstimate(flops=0, bytes_accessed=MIB, transcendentals=0),
        name="split",
    )(keep, got)


def near_kernel(l_ref, first_ref, second_ref, *refs):
    xs, zs, outs = (first_ref,) + refs[:3], (second_ref,) + refs[3:6], refs[6:]
    z, x = lax.axis_index("z"), lax.axis_index("x")
    for n, away in enumerate(RING):
        at = pl.ds(pl.multiple_of(lax.rem(x + away + 4, 4) * 16, 16), 16)
        outs[0][at, :] = xs[n][:, : 2 * RW]
        outs[2][at, :] = xs[n][:, 2 * RW :] if n else l_ref[...]
        at = pl.ds(pl.multiple_of(lax.rem(z + away + 4, 4) * 16, 16), 16)
        outs[1][at, :] = zs[n][...]


def join_near(l, first, second, xs, zs):
    return pl.pallas_call(
        near_kernel,
        out_shape=[jax.ShapeDtypeStruct((64, n), BF16) for n in (2 * RW, 2 * RW, LW)],
        compiler_params=pltpu.CompilerParams(vmem_limit_bytes=16 * MIB),
        cost_estimate=pl.CostEstimate(flops=0, bytes_accessed=2 * MIB, transcendentals=0),
        name="join_near",
    )(l, first, second, *xs, *zs)


def far_kernel(after_ref, *refs):
    z, x = lax.axis_index("z"), lax.axis_index("x")
    for half, at in ((0, z), (1, x)):
        mine, before, behind, across0, across1 = refs[half * 5 : half * 5 + 5]
        out = refs[10 + half]
        rows = [pl.ds(pl.multiple_of(lax.rem(at + away + 4, 4) * 64, 64), 64) for away in RING]
        out[rows[0], :] = mine[...]
        out[rows[1], :] = before[...]
        out[rows[2], :] = behind[...]
        out[rows[3], :RW] = across0[...]
        out[rows[3], RW:] = across1[...]


def join_far(pieces, after):
    return pl.pallas_call(
        far_kernel,
        in_specs=[pl.BlockSpec(memory_space=pl.ANY)] + [pl.BlockSpec(memory_space=pltpu.VMEM)] * 10,
        out_shape=[jax.ShapeDtypeStruct((256, 2 * RW), BF16)] * 2,
        compiler_params=pltpu.CompilerParams(vmem_limit_bytes=24 * MIB),
        cost_estimate=pl.CostEstimate(flops=0, bytes_accessed=8 * MIB, transcendentals=0),
        name="join_far",
    )(after, *pieces)


def left_kernel(l0_ref, l1_ref, l2_ref, l3_ref, wf_ref, bf_ref, lt_ref, kl_ref, wt_ref, bt_ref, l_ref, mix, scr, w_scr):
    for m, ref in enumerate((l0_ref, l1_ref, l2_ref, l3_ref)):
        l_ref[m * 64 : (m + 1) * 64, :] = ref[...]
    y = lax.axis_index("rep")
    place = lambda away: jnp.where(away == 0, 0, jnp.where(away == 3, 1, away + 1))
    for order in range(2):
        for n in range(ZN * XN):
            z, x = (n % ZN, n // ZN) if order else (n // XN, n % XN)
            source = place(lax.rem(z - y + 4, 4)) * 64 + x * 16
            mix[n * 16 : (n + 1) * 16, :] = l_ref[pl.ds(pl.multiple_of(source, 16), 16), :]
        for h in range(2):
            half = slice(h * 128, (h + 1) * 128)
            scr[...] = mix[half, :].astype(F32).T
            for i in range(ROWS):
                lt_ref[order, i * FEAT : (i + 1) * FEAT, half] = scr[pl.ds(i, FEAT, stride=ROWS), :].astype(BF16)
            if order == 0:
                kl_ref[:, half] = scr[FEAT * ROWS : (FEAT + 1) * ROWS, :].astype(BF16)
    w_scr[...] = wf_ref[...].astype(F32)
    for e in range(0, FEAT, 4):
        four = [w_scr[pl.ds(e + k, FEAT, stride=FEAT), :] for k in range(4)]
        wt_ref[:, e * FEAT : (e + 4) * FEAT] = jnp.concatenate(four, axis=0).T.astype(BF16)
    bt_ref[...] = jnp.broadcast_to(bf_ref[...], (OUT, OUT)).T


def arrange_left(pieces, wf, bf):
    return pl.pallas_call(
        left_kernel,
        out_shape=[
            jax.ShapeDtypeStruct((2, ROWS * FEAT, 256), BF16),
            jax.ShapeDtypeStruct((ROWS, 256), BF16),
            jax.ShapeDtypeStruct((OUT, FEAT * FEAT), BF16),
            jax.ShapeDtypeStruct((OUT, OUT), F32),
        ],
        scratch_shapes=[
            pltpu.VMEM((256, LW), BF16),
            pltpu.VMEM((256, LW), BF16),
            pltpu.VMEM((LW, 128), F32),
            pltpu.VMEM((FEAT * FEAT, OUT), F32),
        ],
        compiler_params=pltpu.CompilerParams(vmem_limit_bytes=32 * MIB),
        cost_estimate=pl.CostEstimate(flops=1_000_000, bytes_accessed=3 * MIB, transcendentals=0),
        name="arrange_left",
    )(*pieces, wf, bf)


def pair_kernel(ib, q_ref, lt_ref, kl_ref, r0_ref, r1_ref, w_ref, b_ref, *rest):
    o_ref, scr, rcp = rest[-3:]
    step = pl.program_id(1)

    @pl.when(step == 0)
    def _():
        counts = jnp.dot(kl_ref[...], r0_ref[:, HALF * CB :], preferred_element_type=F32)
        rcp[...] = 1.0 / jnp.maximum(counts, 1.0)

    for half, r_ref in enumerate((r0_ref, r1_ref)):
        o = jnp.dot(lt_ref[half], r_ref[:, : HALF * CB], preferred_element_type=F32).astype(BF16)
        for i in range(ib):
            for e in range(HALF):
                row = (half * HALF + e) * FEAT
                scr[row : row + FEAT, i * CB : (i + 1) * CB] = o[i * FEAT : (i + 1) * FEAT, e * CB : (e + 1) * CB]
    p = jnp.dot(w_ref[...], scr[...], preferred_element_type=F32)
    for i in range(ib):
        scale = rcp[pl.ds(step * ib + i, 1), :]
        o_ref[i] = ((p[:, i * CB : (i + 1) * CB] + b_ref[...]) * scale).T.astype(BF16)


def pair_block(core, lt, kl, r, w, bias, out, ib=64):
    specs = [
        pl.BlockSpec((2, ib * FEAT, 256), lambda k, i, core: (0, i, 0)),
        pl.BlockSpec((ROWS, 256), lambda k, i, core: (0, 0)),
        pl.BlockSpec((256, RW), lambda k, i, core: (0, k)),
        pl.BlockSpec((256, RW), lambda k, i, core: (0, k)),
        pl.BlockSpec((OUT, FEAT * FEAT), lambda k, i, core: (0, 0)),
        pl.BlockSpec((OUT, OUT), lambda k, i, core: (0, 0)),
    ]
    args = [core, lt, kl, *r, w, bias]
    aliases = {}
    if out is not None:
        specs.append(pl.BlockSpec(memory_space=pl.ANY))
        args.append(out)
        aliases = {7: 0}
    return pl.pallas_call(
        functools.partial(pair_kernel, ib),
        grid_spec=pltpu.PrefetchScalarGridSpec(
            num_scalar_prefetch=1,
            grid=(2, ROWS // ib),
            in_specs=specs,
            out_specs=pl.BlockSpec((ib, CB, OUT), lambda k, i, core: (i, core[0] * 2 + k, 0)),
            scratch_shapes=[
                pltpu.VMEM((FEAT * FEAT, ib * CB), BF16),
                pltpu.VMEM((ROWS, CB), F32),
            ],
        ),
        out_shape=jax.ShapeDtypeStruct((ROWS, COLS, OUT), BF16),
        input_output_aliases=aliases,
        compiler_params=pltpu.CompilerParams(vmem_limit_bytes=40 * MIB),
        cost_estimate=pl.CostEstimate(
            flops=4 * ROWS * CB * FEAT * FEAT * (256 + OUT), bytes_accessed=12 * MIB, transcendentals=0
        ),
        name="pair_block",
    )(*args)


def shift(v, axis, by):
    return lax.ppermute(v, axis, [(i, (i + by) % 4) for i in range(4)])


def ring(v, axis):
    return [v] + [shift(v, axis, -away) for away in RING[1:]]


def ring_onward(v, before, behind, axis):
    return [v, before, behind, shift(before[:, :RW], axis, 1), shift(behind[:, RW:], axis, -1)]


def per_device(x, pres, gen, scale, offset, w1, b1, w2, b2, wf, bf):
    core = lax.axis_index("core")
    rep = lax.axis_index("rep").astype(jnp.int32).reshape(1)
    keep, send = prepare(
        rep,
        x,
        pres,
        gen.reshape(1, -1),
        scale.reshape(1, -1),
        offset.reshape(1, -1),
        w1.T,
        b1.reshape(1, -1),
        w2.T,
        b2.reshape(1, -1),
    )
    swap = lambda v: lax.ppermute(v, "core", [(0, 1), (1, 0)])
    l, first, second, *xs = split(keep, swap(send))
    xs = [shift(v, "x", -away) for v, away in zip(xs, RING[1:])]
    near0, near1, l = join_near(l, first, second, xs, ring(second, "z")[1:])
    l = lax.ppermute(l, ("z", "rep"), [(z * 4 + y, y * 4 + z) for z in range(4) for y in range(4)])
    sides0 = [shift(near0, "z", 1), shift(near0, "z", -1)]
    sides1 = [shift(near1, "x", 1), shift(near1, "x", -1)]
    l = lax.optimization_barrier((l, *sides0, *sides1))[0]
    lt, kl, wt, bt = arrange_left(ring(l, "rep"), wf, bf.reshape(1, -1))
    own = join_far(ring_onward(near0, *sides0, "z") + ring_onward(near1, *sides1, "x"), kl)
    other = [swap(v) for v in own]
    out = pair_block(core.astype(jnp.int32).reshape(1), lt, kl, own, wt, bt, None)
    return pair_block((1 - core).astype(jnp.int32).reshape(1), lt, kl, other, wt, bt, out)


def solution(mesh):
    grid = Mesh(mesh.devices.reshape(ZN, XN, CN, YN), ("z", "x", "core", "rep"))
    dap = ("z", "x", "core")
    in_specs = (P(dap, "rep", None), P(dap, "rep"), P(), P(), P(), P(), P(), P(), P(), P(), P())
    return jax.shard_map(
        per_device, mesh=grid, in_specs=in_specs, out_specs=P(dap, "rep", None), check_vma=False
    )
```

time: 196 us -> 111 us (0.57)
  waiting for transfers between devices: 111 us -> 36.6 us
  starting transfers between devices: 0.76 us -> 25.5 us
  blocking collectives: 15.9 us -> 0 us
  between operations: 13.2 us -> 0.13 us
  local copies, waits for them, and re-layouts: 8.4 us -> 2.64 us
    all_gather x3 -> x0, waiting for transfers between devices: 110 us -> none  [the longest x2 85.5 us: gather_chips(): return lax.all_gather(v, ('z', 'x'), axis=0, tiled=True)]
    ppermute x2 -> x20, waiting for transfers between devices: 0.01 us -> 36.6 us  [the longest x17 34.8 us: shift(): return lax.ppermute(v, axis, [(i, (i + by) % 4) for i in range(4)])]
    ppermute x2 -> x20, starting transfers between devices: 0.01 us -> 24.9 us  [the longest x17 24.3 us: shift(): return lax.ppermute(v, axis, [(i, (i + by) % 4) for i in range(4)])]
    all_to_all x2 -> x0, blocking collectives: 15.9 us -> none  [the longest x1 12 us: per_device(): lax.all_to_all(l, ('x', 'core'), split_axis=0, concat_axis=0, tiled=True)]
    unnamed x20 -> x10, local copies, waits for them, and re-layouts: 7.2 us -> 2.56 us
    pallas_call x5 -> x6, Pallas kernels: 41.8 us -> 38.4 us  [the longest x2 33 us: pair_block(): pl.pallas_call(functools.partial(pair_kernel, ib), grid_spec=pltpu.Prefet...]
    pallas_call x1, Pallas kernels: 3.34 us -> 5.71 us  [prepare(): pl.pallas_call(prepare_kernel, grid_spec=pltpu.PrefetchScalarGridSpec(num...]
  transfers between devices with their start and end apart: 6 -> 21, of which waited for: 3 -> 10; matrix products, arithmetic and copies ran while one was open for 0% -> 0% of each run, Pallas kernels for 16% -> 18%
where the time goes in v2:
time: 111 us; the launch traced here: 109 us
  Pallas kernels  44.1 us (40%)
  waiting for transfers between devices  36.6 us (33%)
  starting transfers between devices  25.5 us (23%)
  local copies, waits for them, and re-layouts  2.64 us (2%)
    ppermute x17, waiting for transfers between devices, shift(): return lax.ppermute(v, axis, [(i, (i + by) % 4) for i in range(4)])  34.8 us
    pallas_call x2, Pallas kernels, pair_block(): pl.pallas_call(functools.partial(pair_kernel, ib), grid_spec=pltpu.Prefet...  33 us
    ppermute x17, starting transfers between devices, shift(): return lax.ppermute(v, axis, [(i, (i + by) % 4) for i in range(4)])  24.3 us
    pallas_call x1, Pallas kernels, prepare(): pl.pallas_call(prepare_kernel, grid_spec=pltpu.PrefetchScalarGridSpec(num...  5.71 us
    pallas_call x1, Pallas kernels, arrange_left(): pl.pallas_call(left_kernel, out_shape=[jax.ShapeDtypeStruct((2, ROWS * FE...  3.47 us
    unnamed x10, local copies, waits for them, and re-layouts  2.56 us
  transfers between devices with their start and end apart: 21, of which 10 were waited for; matrix products, arithmetic and copies ran while one was open for 0% of the time, Pallas kernels for 18%

profile of v2, /device:TPU:0, one launch (start us, length us, event | category | flops | bytes accessed | tf_op | source)
XLA Modules:
  0.0 109.0 jit_solution(13241441836634072371)
XLA Ops:
  0.0 0.0 copy-start.1
  0.0 5.7 %prepare.1 = (bf16[8,17408]{1,0:T(8,128)(2,1)}, bf16[8,17408]{1,0:T(8,128)(2,1)}) custom-call(s32[1]{0:T(128)} %bitcast.1.rep_ref, bf16[8,512,256]{2,1,0:T(8,128)(2,1)} %x_ref.1, bf16[8,512]{1,0:T(8,128)(2,1)} %pres_ref.1, s32[1,2048]{1,0:T(1,128)} %bitcast.14, f32[1,256]{1,0:T(1,128)} %bitcast.15, f32[1,256]{1,0:T(1,128)} %bitcast.16, ...), custom_call_target="tpu_custom_call" | custom-call | flops 140000000 | bytes 3145728 | tf_op jit(solution)/shard_map/prepare/pallas_call | solution.py:84
  5.7 0.0 copy-start.2
  5.7 0.0 collective-permute-start
  5.8 1.8 %collective-permute-done.got_ref = bf16[8,17408]{1,0:T(8,128)(2,1)S(1)} collective-permute-done((bf16[8,17408]{1,0:T(8,128)(2,1)}, bf16[8,17408]{1,0:T(8,128)(2,1)S(1)}, u32[]{:S(2)}, u32[]{:S(2)}) %collective-permute-start) | collective-permute-done | bytes 278560 | tf_op jit(solution)/shard_map/ppermute | solution.py:319
  7.5 0.0 copy-start
  7.5 1.0 copy-done
  8.5 0.1 split.1
  8.6 4.1 %collective-permute-start.6 = (bf16[16,4352]{1,0:T(8,128)(2,1)S(1)}, bf16[16,4352]{1,0:T(8,128)(2,1)S(1)}, u32[]{:S(2)}, u32[]{:S(2)}) collective-permute-start(bf16[16,4352]{1,0:T(8,128)(2,1)S(1)} %get-tuple-element.27.second_ref), channel_id=1, source_target_pairs={{0,64},{32,96},{64,0},{96,32},{1,65},{33,97},{65,1},{97,33},{2,66}... | collective-permute-start | bytes 417800 | tf_op jit(solution)/shard_map/ppermute | solution.py:293
  12.7 1.5 %collective-permute-start.1 = (bf16[16,6528]{1,0:T(8,128)(2,1)S(1)}, bf16[16,6528]{1,0:T(8,128)(2,1)S(1)}, u32[]{:S(2)}, u32[]{:S(2)}) collective-permute-start(bf16[16,6528]{1,0:T(8,128)(2,1)S(1)} %get-tuple-element.28), channel_id=1, source_target_pairs={{0,8},{8,16},{16,24},{24,0},{1,9},{9,17},{17,25},{25,1},{2,10},{10... | collective-permute-start | bytes 626696 | tf_op jit(solution)/shard_map/ppermute | solution.py:293
  14.1 1.7 %collective-permute-start.2 = (bf16[16,6528]{1,0:T(8,128)(2,1)S(1)}, bf16[16,6528]{1,0:T(8,128)(2,1)S(1)}, u32[]{:S(2)}, u32[]{:S(2)}) collective-permute-start(bf16[16,6528]{1,0:T(8,128)(2,1)S(1)} %get-tuple-element.29), channel_id=1, source_target_pairs={{0,24},{8,0},{16,8},{24,16},{1,25},{9,1},{17,9},{25,17},{2,26},{10... | collective-permute-start | bytes 626696 | tf_op jit(solution)/shard_map/ppermute | solution.py:293
  15.9 1.8 %collective-permute-start.3 = (bf16[16,6528]{1,0:T(8,128)(2,1)S(1)}, bf16[16,6528]{1,0:T(8,128)(2,1)S(1)}, u32[]{:S(2)}, u32[]{:S(2)}) collective-permute-start(bf16[16,6528]{1,0:T(8,128)(2,1)S(1)} %get-tuple-element.30), channel_id=1, source_target_pairs={{0,16},{8,24},{16,0},{24,8},{1,17},{9,25},{17,1},{25,9},{2,18},{10... | collective-permute-start | bytes 626696 | tf_op jit(solution)/shard_map/ppermute | solution.py:293
  17.7 0.7 collective-permute-start.5
  18.4 0.0 collective-permute-done.6.refs_5_
  18.4 1.3 %collective-permute-start.4 = (bf16[16,4352]{1,0:T(8,128)(2,1)S(1)}, bf16[16,4352]{1,0:T(8,128)(2,1)S(1)}, u32[]{:S(2)}, u32[]{:S(2)}) collective-permute-start(bf16[16,4352]{1,0:T(8,128)(2,1)S(1)} %get-tuple-element.27.second_ref), channel_id=1, source_target_pairs={{0,32},{32,64},{64,96},{96,0},{1,33},{33,65},{65,97},{97,1},{2,34}... | collective-permute-start | bytes 417800 | tf_op jit(solution)/shard_map/ppermute | solution.py:293
  19.7 3.0 %collective-permute-done.5.refs_4_ = bf16[16,4352]{1,0:T(8,128)(2,1)S(1)} collective-permute-done((bf16[16,4352]{1,0:T(8,128)(2,1)S(1)}, bf16[16,4352]{1,0:T(8,128)(2,1)S(1)}, u32[]{:S(2)}, u32[]{:S(2)}) %collective-permute-start.5) | collective-permute-done | bytes 139296 | tf_op jit(solution)/shard_map/ppermute | solution.py:293
  22.8 1.9 %collective-permute-done.4.refs_3_ = bf16[16,4352]{1,0:T(8,128)(2,1)S(1)} collective-permute-done((bf16[16,4352]{1,0:T(8,128)(2,1)S(1)}, bf16[16,4352]{1,0:T(8,128)(2,1)S(1)}, u32[]{:S(2)}, u32[]{:S(2)}) %collective-permute-start.4) | collective-permute-done | bytes 139296 | tf_op jit(solution)/shard_map/ppermute | solution.py:293
  24.7 0.0 collective-permute-done.1.refs_0_
  24.7 0.0 collective-permute-done.2.refs_1_
  24.7 1.6 %collective-permute-done.3.refs_2_ = bf16[16,6528]{1,0:T(8,128)(2,1)S(1)} collective-permute-done((bf16[16,6528]{1,0:T(8,128)(2,1)S(1)}, bf16[16,6528]{1,0:T(8,128)(2,1)S(1)}, u32[]{:S(2)}, u32[]{:S(2)}) %collective-permute-start.3) | collective-permute-done | bytes 208928 | tf_op jit(solution)/shard_map/ppermute | solution.py:293
  26.3 0.1 join_near.1
  26.4 0.8 collective-permute-start.9
  27.1 1.3 %collective-permute-start.8 = (bf16[64,4352]{1,0:T(8,128)(2,1)S(1)}, bf16[64,4352]{1,0:T(8,128)(2,1)S(1)}, u32[]{:S(2)}, u32[]{:S(2)}) collective-permute-start(bf16[64,4352]{1,0:T(8,128)(2,1)S(1)} %get-tuple-element.32.refs_0_), channel_id=1, source_target_pairs={{0,32},{32,64},{64,96},{96,0},{1,33},{33,65},{65,97},{97,1},{2,34}... | collective-permute-start | bytes 1671176 | tf_op jit(solution)/shard_map/ppermute | solution.py:293
  28.5 2.0 %collective-permute-start.11 = (bf16[64,4352]{1,0:T(8,128)(2,1)S(1)}, bf16[64,4352]{1,0:T(8,128)(2,1)S(1)}, u32[]{:S(2)}, u32[]{:S(2)}) collective-permute-start(bf16[64,4352]{1,0:T(8,128)(2,1)S(1)} %get-tuple-element.33.refs_5_), channel_id=1, source_target_pairs={{0,24},{8,0},{16,8},{24,16},{1,25},{9,1},{17,9},{25,17},{2,26},{10... | collective-permute-start | bytes 1671176 | tf_op jit(solution)/shard_map/ppermute | solution.py:293
  30.4 0.1 collective-permute-start.10
  30.5 0.7 collective-permute-start.7
  31.2 0.0 collective-permute-done.7.l0_ref
  31.2 8.8 %collective-permute-done.9.refs_2_ = bf16[64,4352]{1,0:T(8,128)(2,1)S(1)} collective-permute-done((bf16[64,4352]{1,0:T(8,128)(2,1)S(1)}, bf16[64,4352]{1,0:T(8,128)(2,1)S(1)}, u32[]{:S(2)}, u32[]{:S(2)}) %collective-permute-start.9) | collective-permute-done | bytes 557088 | tf_op jit(solution)/shard_map/ppermute | solution.py:293
  39.9 11.2 %collective-permute-done.8.refs_1_ = bf16[64,4352]{1,0:T(8,128)(2,1)S(1)} collective-permute-done((bf16[64,4352]{1,0:T(8,128)(2,1)S(1)}, bf16[64,4352]{1,0:T(8,128)(2,1)S(1)}, u32[]{:S(2)}, u32[]{:S(2)}) %collective-permute-start.8) | collective-permute-done | bytes 557088 | tf_op jit(solution)/shard_map/ppermute | solution.py:293
  51.1 0.0 collective-permute-done.11.refs_7_
  51.2 0.0 collective-permute-done.10.refs_6_
  51.2 0.0 collective-permute-start.14
  51.2 5.1 %collective-permute-start.13 = (bf16[64,2176]{1,0:T(8,128)(2,1)S(1)}, bf16[64,2176]{1,0:T(8,128)(2,1)S(1)}, u32[]{:S(2)}, u32[]{:S(2)}) collective-permute-start(bf16[64,2176]{1,0:T(8,128)(2,1)S(1)} %collective-permute-done.7.l0_ref), channel_id=1, source_target_pairs={{0,3},{1,0},{2,1},{3,2},{4,7},{5,4},{6,5},{7,6},{8,11},{9,8},{10,9... | collective-permute-start | bytes 835592 | tf_op jit(solution)/shard_map/ppermute | solution.py:293
  56.2 0.0 collective-permute-start.12
  56.3 2.6 %collective-permute-start.16 = (bf16[64,2176]{1,0:T(8,128)(2,1)S(1)}, bf16[64,2176]{1,0:T(8,128)(2,1)S(1)}, u32[]{:S(2)}, u32[]{:S(2)}) collective-permute-start(bf16[64,2176]{1,0:T(8,128)(2,1)S(1)} %slice.17), channel_id=1, source_target_pairs={{0,96},{32,0},{64,32},{96,64},{1,97},{33,1},{65,33},{97,65},{2,98}... | collective-permute-start | bytes 835592 | tf_op jit(solution)/shard_map/ppermute | solution.py:293
  58.9 0.1 collective-permute-start.15
  59.0 3.1 %collective-permute-done.14.l3_ref = bf16[64,2176]{1,0:T(8,128)(2,1)S(1)} collective-permute-done((bf16[64,2176]{1,0:T(8,128)(2,1)S(1)}, bf16[64,2176]{1,0:T(8,128)(2,1)S(1)}, u32[]{:S(2)}, u32[]{:S(2)}) %collective-permute-start.14) | collective-permute-done | bytes 278560 | tf_op jit(solution)/shard_map/ppermute | solution.py:293
  62.1 0.8 collective-permute-start.18
  63.0 1.4 %collective-permute-done.13.l2_ref = bf16[64,2176]{1,0:T(8,128)(2,1)S(1)} collective-permute-done((bf16[64,2176]{1,0:T(8,128)(2,1)S(1)}, bf16[64,2176]{1,0:T(8,128)(2,1)S(1)}, u32[]{:S(2)}, u32[]{:S(2)}) %collective-permute-start.13) | collective-permute-done | bytes 278560 | tf_op jit(solution)/shard_map/ppermute | solution.py:293
  64.4 0.5 collective-permute-start.17
  64.9 0.9 collective-permute-done.12.l1_ref
  65.8 0.0 copy-done.1
  65.8 0.0 copy-done.2
  65.8 3.5 %arrange_left.1 = (bf16[2,2048,256]{2,1,0:T(8,128)(2,1)S(1)}, bf16[64,256]{1,0:T(8,128)(2,1)S(1)}, bf16[128,1024]{1,0:T(8,128)(2,1)S(1)}, f32[128,128]{1,0:T(8,128)S(1)}) custom-call(bf16[64,2176]{1,0:T(8,128)(2,1)S(1)} %collective-permute-done.7.l0_ref, bf16[64,2176]{1,0:T(8,128)(2,1)S(1)} %collective-permute-done.12.l1_ref, ...), custom_call_target="tpu_custom_call" | custom-call | flops 1000000 | bytes 3145728 | tf_op jit(solution)/shard_map/arrange_left/pallas_call | solution.py:214
  69.3 0.0 copy-start.3
  69.3 0.0 collective-permute-done.16.refs_4_
  69.3 0.0 collective-permute-done.15.refs_3_
  69.3 0.0 collective-permute-done.18.refs_9_
  69.4 2.8 %collective-permute-done.17.refs_8_ = bf16[64,2176]{1,0:T(8,128)(2,1)S(1)} collective-permute-done((bf16[64,2176]{1,0:T(8,128)(2,1)S(1)}, bf16[64,2176]{1,0:T(8,128)(2,1)S(1)}, u32[]{:S(2)}, u32[]{:S(2)}) %collective-permute-start.17) | collective-permute-done | bytes 278560 | tf_op jit(solution)/shard_map/ppermute | solution.py:293
  72.2 1.7 %join_far.1 = (bf16[256,4352]{1,0:T(8,128)(2,1)}, bf16[256,4352]{1,0:T(8,128)(2,1)S(1)}) custom-call(bf16[64,256]{1,0:T(8,128)(2,1)S(1)} %get-tuple-element.36.after_ref.kl_ref, bf16[64,4352]{1,0:T(8,128)(2,1)S(1)} %get-tuple-element.32.refs_0_, bf16[64,4352]{1,0:T(8,128)(2,1)S(1)} %collective-permute-done.8.refs_1_, ...), custom_call_target="tpu_custom_call" | custom-call | bytes 8388608 | tf_op jit(solution)/shard_map/join_far/pallas_call | solution.py:179
  73.9 0.0 copy-done.3
  73.9 0.0 collective-permute-start.19
  73.9 0.5 collective-permute-start.20
  74.4 0.0 copy-start.4
  74.4 1.6 %copy-done.4 = bf16[2,2048,256]{2,1,0:T(8,128)(2,1)S(1)} copy-done((bf16[2,2048,256]{2,1,0:T(8,128)(2,1)S(1)}, bf16[2,2048,256]{2,1,0:T(8,128)(2,1)}, u32[]{:S(2)}) %copy-start.4) | copy-done | bytes 2097176
  76.0 16.2 %pair_block.2.rest_0_ = bf16[64,512,128]{2,1,0:T(8,128)(2,1)} custom-call(s32[1]{0:T(128)} %bitcast.10.q_ref, bf16[2,2048,256]{2,1,0:T(8,128)(2,1)S(1)} %copy-done.4, bf16[64,256]{1,0:T(8,128)(2,1)S(1)} %get-tuple-element.36.after_ref.kl_ref, bf16[256,4352]{1,0:T(8,128)(2,1)} %get-tuple-element.37.r0_ref, bf16[256,4352]{1,0:T(8,128)(2,1)S(1)} %get-tuple-element.38.r1_ref, ...), custom_call_target="tpu_custom_call" | custom-call | flops 12884901888 | bytes 12582912 | tf_op jit(solution)/shard_map/pair_block/pallas_call | solution.py:270
  92.2 0.0 collective-permute-done.19.r0_ref
  92.2 0.0 collective-permute-done.20.r1_ref
  92.2 16.8 %pair_block.3 = bf16[64,512,128]{2,1,0:T(8,128)(2,1)} custom-call(s32[1]{0:T(128)} %bitcast.q_ref, bf16[2,2048,256]{2,1,0:T(8,128)(2,1)S(1)} %copy-done.4, bf16[64,256]{1,0:T(8,128)(2,1)S(1)} %get-tuple-element.36.after_ref.kl_ref, bf16[256,4352]{1,0:T(8,128)(2,1)} %collective-permute-done.19.r0_ref, ...), custom_call_target="tpu_custom_call", output_to_operand_aliasing={{}: (7, {})} | custom-call | flops 12884901888 | bytes 12582912 | tf_op jit(solution)/shard_map/pair_block/pallas_call | solution.py:270
  (4 shorter events, 0.1 us)
Async XLA Ops:
  0.0 65.8 %copy-start.1 = (bf16[1024,128]{1,0:T(8,128)(2,1)S(1)}, bf16[1024,128]{1,0:T(8,128)(2,1)}, u32[]{:S(2)}) copy-start(bf16[1024,128]{1,0:T(8,128)(2,1)} %wf_ref.1) | copy-start | bytes 786436
  5.7 60.1 %copy-start.2 = (f32[128]{0:T(128)S(1)}, f32[128]{0:T(128)}, u32[]{:S(2)}) copy-start(f32[128]{0:T(128)} %param.21) | copy-start | bytes 1540
  5.7 1.8 %collective-permute-start = (bf16[8,17408]{1,0:T(8,128)(2,1)}, bf16[8,17408]{1,0:T(8,128)(2,1)S(1)}, u32[]{:S(2)}, u32[]{:S(2)}) collective-permute-start(bf16[8,17408]{1,0:T(8,128)(2,1)} %get-tuple-element.24), channel_id=1, source_target_pairs={{0,4},{4,0},{1,5},{5,1},{2,6},{6,2},{3,7},{7,3},{8,12},{12,8},{9,1... | collective-permute-start | bytes 835592 | tf_op jit(solution)/shard_map/ppermute | solution.py:319
  7.5 1.0 copy-start
  8.6 9.8 %collective-permute-start.6 = (bf16[16,4352]{1,0:T(8,128)(2,1)S(1)}, bf16[16,4352]{1,0:T(8,128)(2,1)S(1)}, u32[]{:S(2)}, u32[]{:S(2)}) collective-permute-start(bf16[16,4352]{1,0:T(8,128)(2,1)S(1)} %get-tuple-element.27.second_ref), channel_id=1, source_target_pairs={{0,64},{32,96},{64,0},{96,32},{1,65},{33,97},{65,1},{97,33},{2,66}... | collective-permute-start | bytes 417800 | tf_op jit(solution)/shard_map/ppermute | solution.py:293
  12.7 12.0 %collective-permute-start.1 = (bf16[16,6528]{1,0:T(8,128)(2,1)S(1)}, bf16[16,6528]{1,0:T(8,128)(2,1)S(1)}, u32[]{:S(2)}, u32[]{:S(2)}) collective-permute-start(bf16[16,6528]{1,0:T(8,128)(2,1)S(1)} %get-tuple-element.28), channel_id=1, source_target_pairs={{0,8},{8,16},{16,24},{24,0},{1,9},{9,17},{17,25},{25,1},{2,10},{10... | collective-permute-start | bytes 626696 | tf_op jit(solution)/shard_map/ppermute | solution.py:293
  14.1 10.6 %collective-permute-start.2 = (bf16[16,6528]{1,0:T(8,128)(2,1)S(1)}, bf16[16,6528]{1,0:T(8,128)(2,1)S(1)}, u32[]{:S(2)}, u32[]{:S(2)}) collective-permute-start(bf16[16,6528]{1,0:T(8,128)(2,1)S(1)} %get-tuple-element.29), channel_id=1, source_target_pairs={{0,24},{8,0},{16,8},{24,16},{1,25},{9,1},{17,9},{25,17},{2,26},{10... | collective-permute-start | bytes 626696 | tf_op jit(solution)/shard_map/ppermute | solution.py:293
  15.9 10.4 %collective-permute-start.3 = (bf16[16,6528]{1,0:T(8,128)(2,1)S(1)}, bf16[16,6528]{1,0:T(8,128)(2,1)S(1)}, u32[]{:S(2)}, u32[]{:S(2)}) collective-permute-start(bf16[16,6528]{1,0:T(8,128)(2,1)S(1)} %get-tuple-element.30), channel_id=1, source_target_pairs={{0,16},{8,24},{16,0},{24,8},{1,17},{9,25},{17,1},{25,9},{2,18},{10... | collective-permute-start | bytes 626696 | tf_op jit(solution)/shard_map/ppermute | solution.py:293
  17.7 5.1 %collective-permute-start.5 = (bf16[16,4352]{1,0:T(8,128)(2,1)S(1)}, bf16[16,4352]{1,0:T(8,128)(2,1)S(1)}, u32[]{:S(2)}, u32[]{:S(2)}) collective-permute-start(bf16[16,4352]{1,0:T(8,128)(2,1)S(1)} %get-tuple-element.27.second_ref), channel_id=1, source_target_pairs={{0,96},{32,0},{64,32},{96,64},{1,97},{33,1},{65,33},{97,65},{2,98}... | collective-permute-start | bytes 417800 | tf_op jit(solution)/shard_map/ppermute | solution.py:293
  18.4 6.3 %collective-permute-start.4 = (bf16[16,4352]{1,0:T(8,128)(2,1)S(1)}, bf16[16,4352]{1,0:T(8,128)(2,1)S(1)}, u32[]{:S(2)}, u32[]{:S(2)}) collective-permute-start(bf16[16,4352]{1,0:T(8,128)(2,1)S(1)} %get-tuple-element.27.second_ref), channel_id=1, source_target_pairs={{0,32},{32,64},{64,96},{96,0},{1,33},{33,65},{65,97},{97,1},{2,34}... | collective-permute-start | bytes 417800 | tf_op jit(solution)/shard_map/ppermute | solution.py:293
  26.4 13.6 %collective-permute-start.9 = (bf16[64,4352]{1,0:T(8,128)(2,1)S(1)}, bf16[64,4352]{1,0:T(8,128)(2,1)S(1)}, u32[]{:S(2)}, u32[]{:S(2)}) collective-permute-start(bf16[64,4352]{1,0:T(8,128)(2,1)S(1)} %get-tuple-element.32.refs_0_), channel_id=1, source_target_pairs={{0,96},{32,0},{64,32},{96,64},{1,97},{33,1},{65,33},{97,65},{2,98}... | collective-permute-start | bytes 1671176 | tf_op jit(solution)/shard_map/ppermute | solution.py:293
  27.1 24.0 %collective-permute-start.8 = (bf16[64,4352]{1,0:T(8,128)(2,1)S(1)}, bf16[64,4352]{1,0:T(8,128)(2,1)S(1)}, u32[]{:S(2)}, u32[]{:S(2)}) collective-permute-start(bf16[64,4352]{1,0:T(8,128)(2,1)S(1)} %get-tuple-element.32.refs_0_), channel_id=1, source_target_pairs={{0,32},{32,64},{64,96},{96,0},{1,33},{33,65},{65,97},{97,1},{2,34}... | collective-permute-start | bytes 1671176 | tf_op jit(solution)/shard_map/ppermute | solution.py:293
  28.5 22.7 %collective-permute-start.11 = (bf16[64,4352]{1,0:T(8,128)(2,1)S(1)}, bf16[64,4352]{1,0:T(8,128)(2,1)S(1)}, u32[]{:S(2)}, u32[]{:S(2)}) collective-permute-start(bf16[64,4352]{1,0:T(8,128)(2,1)S(1)} %get-tuple-element.33.refs_5_), channel_id=1, source_target_pairs={{0,24},{8,0},{16,8},{24,16},{1,25},{9,1},{17,9},{25,17},{2,26},{10... | collective-permute-start | bytes 1671176 | tf_op jit(solution)/shard_map/ppermute | solution.py:293
  30.4 20.7 %collective-permute-start.10 = (bf16[64,4352]{1,0:T(8,128)(2,1)S(1)}, bf16[64,4352]{1,0:T(8,128)(2,1)S(1)}, u32[]{:S(2)}, u32[]{:S(2)}) collective-permute-start(bf16[64,4352]{1,0:T(8,128)(2,1)S(1)} %get-tuple-element.33.refs_5_), channel_id=1, source_target_pairs={{0,8},{8,16},{16,24},{24,0},{1,9},{9,17},{17,25},{25,1},{2,10},{10... | collective-permute-start | bytes 1671176 | tf_op jit(solution)/shard_map/ppermute | solution.py:293
  30.5 0.7 collective-permute-start.7
  51.2 11.0 %collective-permute-start.14 = (bf16[64,2176]{1,0:T(8,128)(2,1)S(1)}, bf16[64,2176]{1,0:T(8,128)(2,1)S(1)}, u32[]{:S(2)}, u32[]{:S(2)}) collective-permute-start(bf16[64,2176]{1,0:T(8,128)(2,1)S(1)} %collective-permute-done.7.l0_ref), channel_id=1, source_target_pairs={{0,2},{1,3},{2,0},{3,1},{4,6},{5,7},{6,4},{7,5},{8,10},{9,11},{10,... | collective-permute-start | bytes 835592 | tf_op jit(solution)/shard_map/ppermute | solution.py:293
  51.2 13.2 %collective-permute-start.13 = (bf16[64,2176]{1,0:T(8,128)(2,1)S(1)}, bf16[64,2176]{1,0:T(8,128)(2,1)S(1)}, u32[]{:S(2)}, u32[]{:S(2)}) collective-permute-start(bf16[64,2176]{1,0:T(8,128)(2,1)S(1)} %collective-permute-done.7.l0_ref), channel_id=1, source_target_pairs={{0,3},{1,0},{2,1},{3,2},{4,7},{5,4},{6,5},{7,6},{8,11},{9,8},{10,9... | collective-permute-start | bytes 835592 | tf_op jit(solution)/shard_map/ppermute | solution.py:293
  56.2 9.6 %collective-permute-start.12 = (bf16[64,2176]{1,0:T(8,128)(2,1)S(1)}, bf16[64,2176]{1,0:T(8,128)(2,1)S(1)}, u32[]{:S(2)}, u32[]{:S(2)}) collective-permute-start(bf16[64,2176]{1,0:T(8,128)(2,1)S(1)} %collective-permute-done.7.l0_ref), channel_id=1, source_target_pairs={{0,1},{1,2},{2,3},{3,0},{4,5},{5,6},{6,7},{7,4},{8,9},{9,10},{10,1... | collective-permute-start | bytes 835592 | tf_op jit(solution)/shard_map/ppermute | solution.py:293
  56.3 13.1 %collective-permute-start.16 = (bf16[64,2176]{1,0:T(8,128)(2,1)S(1)}, bf16[64,2176]{1,0:T(8,128)(2,1)S(1)}, u32[]{:S(2)}, u32[]{:S(2)}) collective-permute-start(bf16[64,2176]{1,0:T(8,128)(2,1)S(1)} %slice.17), channel_id=1, source_target_pairs={{0,96},{32,0},{64,32},{96,64},{1,97},{33,1},{65,33},{97,65},{2,98}... | collective-permute-start | bytes 835592 | tf_op jit(solution)/shard_map/ppermute | solution.py:293
  58.9 10.5 %collective-permute-start.15 = (bf16[64,2176]{1,0:T(8,128)(2,1)S(1)}, bf16[64,2176]{1,0:T(8,128)(2,1)S(1)}, u32[]{:S(2)}, u32[]{:S(2)}) collective-permute-start(bf16[64,2176]{1,0:T(8,128)(2,1)S(1)} %slice.16), channel_id=1, source_target_pairs={{0,32},{32,64},{64,96},{96,0},{1,33},{33,65},{65,97},{97,1},{2,34}... | collective-permute-start | bytes 835592 | tf_op jit(solution)/shard_map/ppermute | solution.py:293
  62.1 7.2 %collective-permute-start.18 = (bf16[64,2176]{1,0:T(8,128)(2,1)S(1)}, bf16[64,2176]{1,0:T(8,128)(2,1)S(1)}, u32[]{:S(2)}, u32[]{:S(2)}) collective-permute-start(bf16[64,2176]{1,0:T(8,128)(2,1)S(1)} %slice.19), channel_id=1, source_target_pairs={{0,24},{8,0},{16,8},{24,16},{1,25},{9,1},{17,9},{25,17},{2,26},{10... | collective-permute-start | bytes 835592 | tf_op jit(solution)/shard_map/ppermute | solution.py:293
  64.4 7.8 %collective-permute-start.17 = (bf16[64,2176]{1,0:T(8,128)(2,1)S(1)}, bf16[64,2176]{1,0:T(8,128)(2,1)S(1)}, u32[]{:S(2)}, u32[]{:S(2)}) collective-permute-start(bf16[64,2176]{1,0:T(8,128)(2,1)S(1)} %slice.18), channel_id=1, source_target_pairs={{0,8},{8,16},{16,24},{24,0},{1,9},{9,17},{17,25},{25,1},{2,10},{10... | collective-permute-start | bytes 835592 | tf_op jit(solution)/shard_map/ppermute | solution.py:293
  69.3 4.6 %copy-start.3 = (bf16[2,2048,256]{2,1,0:T(8,128)(2,1)}, bf16[2,2048,256]{2,1,0:T(8,128)(2,1)S(1)}, u32[]{:S(2)}) copy-start(bf16[2,2048,256]{2,1,0:T(8,128)(2,1)S(1)} %get-tuple-element.35.lt_ref) | copy-start | bytes 6291460
  73.9 18.3 %collective-permute-start.19 = (bf16[256,4352]{1,0:T(8,128)(2,1)}, bf16[256,4352]{1,0:T(8,128)(2,1)}, u32[]{:S(2)}, u32[]{:S(2)}) collective-permute-start(bf16[256,4352]{1,0:T(8,128)(2,1)} %get-tuple-element.37.r0_ref), channel_id=1, source_target_pairs={{0,4},{4,0},{1,5},{5,1},{2,6},{6,2},{3,7},{7,3},{8,12},{12,8},{9,1... | collective-permute-start | bytes 6684680 | tf_op jit(solution)/shard_map/ppermute | solution.py:319
  73.9 18.3 %collective-permute-start.20 = (bf16[256,4352]{1,0:T(8,128)(2,1)S(1)}, bf16[256,4352]{1,0:T(8,128)(2,1)}, u32[]{:S(2)}, u32[]{:S(2)}) collective-permute-start(bf16[256,4352]{1,0:T(8,128)(2,1)S(1)} %get-tuple-element.38.r1_ref), channel_id=1, source_target_pairs={{0,4},{4,0},{1,5},{5,1},{2,6},{6,2},{3,7},{7,3},{8,12},{12,8},{9,1... | collective-permute-start | bytes 6684680 | tf_op jit(solution)/shard_map/ppermute | solution.py:319
  74.4 1.6 %copy-start.4 = (bf16[2,2048,256]{2,1,0:T(8,128)(2,1)S(1)}, bf16[2,2048,256]{2,1,0:T(8,128)(2,1)}, u32[]{:S(2)}) copy-start(bf16[2,2048,256]{2,1,0:T(8,128)(2,1)} %copy-done.3) | copy-start | bytes 6291460

commit v3 on v2

--- a/solution.py
+++ b/solution.py
@@ -186,7 +186,7 @@
     )(after, *pieces)
 
 
-def left_kernel(l0_ref, l1_ref, l2_ref, l3_ref, wf_ref, bf_ref, lt_ref, kl_ref, wt_ref, bt_ref, l_ref, mix, scr, w_scr):
+def left_kernel(l0_ref, l1_ref, l2_ref, l3_ref, lt_ref, kl_ref, l_ref, mix, scr):
     for m, ref in enumerate((l0_ref, l1_ref, l2_ref, l3_ref)):
         l_ref[m * 64 : (m + 1) * 64, :] = ref[...]
     y = lax.axis_index("rep")
@@ -203,6 +203,27 @@
                 lt_ref[order, i * FEAT : (i + 1) * FEAT, half] = scr[pl.ds(i, FEAT, stride=ROWS), :].astype(BF16)
             if order == 0:
                 kl_ref[:, half] = scr[FEAT * ROWS : (FEAT + 1) * ROWS, :].astype(BF16)
+
+
+def arrange_left(pieces):
+    return pl.pallas_call(
+        left_kernel,
+        out_shape=[
+            jax.ShapeDtypeStruct((2, ROWS * FEAT, 256), BF16),
+            jax.ShapeDtypeStruct((ROWS, 256), BF16),
+        ],
+        scratch_shapes=[
+            pltpu.VMEM((256, LW), BF16),
+            pltpu.VMEM((256, LW), BF16),
+            pltpu.VMEM((LW, 128), F32),
+        ],
+        compiler_params=pltpu.CompilerParams(vmem_limit_bytes=32 * MIB),
+        cost_estimate=pl.CostEstimate(flops=1_000_000, bytes_accessed=3 * MIB, transcendentals=0),
+        name="arrange_left",
+    )(*pieces)
+
+
+def weights_kernel(after_ref, wf_ref, bf_ref, wt_ref, bt_ref, w_scr):
     w_scr[...] = wf_ref[...].astype(F32)
     for e in range(0, FEAT, 4):
         four = [w_scr[pl.ds(e + k, FEAT, stride=FEAT), :] for k in range(4)]
@@ -210,25 +231,16 @@
     bt_ref[...] = jnp.broadcast_to(bf_ref[...], (OUT, OUT)).T
 
 
-def arrange_left(pieces, wf, bf):
-    return pl.pallas_call(
-        left_kernel,
-        out_shape=[
-            jax.ShapeDtypeStruct((2, ROWS * FEAT, 256), BF16),
-            jax.ShapeDtypeStruct((ROWS, 256), BF16),
-            jax.ShapeDtypeStruct((OUT, FEAT * FEAT), BF16),
-            jax.ShapeDtypeStruct((OUT, OUT), F32),
-        ],
-        scratch_shapes=[
-            pltpu.VMEM((256, LW), BF16),
-            pltpu.VMEM((256, LW), BF16),
-            pltpu.VMEM((LW, 128), F32),
-            pltpu.VMEM((FEAT * FEAT, OUT), F32),
-        ],
-        compiler_params=pltpu.CompilerParams(vmem_limit_bytes=32 * MIB),
-        cost_estimate=pl.CostEstimate(flops=1_000_000, bytes_accessed=3 * MIB, transcendentals=0),
-        name="arrange_left",
-    )(*pieces, wf, bf)
+def arrange_weights(wf, bf, after):
+    return pl.pallas_call(
+        weights_kernel,
+        in_specs=[pl.BlockSpec(memory_space=pl.ANY)] + [pl.BlockSpec(memory_space=pltpu.VMEM)] * 2,
+        out_shape=[jax.ShapeDtypeStruct((OUT, FEAT * FEAT), BF16), jax.ShapeDtypeStruct((OUT, OUT), F32)],
+        scratch_shapes=[pltpu.VMEM((FEAT * FEAT, OUT), F32)],
+        compiler_params=pltpu.CompilerParams(vmem_limit_bytes=16 * MIB),
+        cost_estimate=pl.CostEstimate(flops=1_000_000, bytes_accessed=MIB, transcendentals=0),
+        name="arrange_weights",
+    )(after, wf, bf)
 
 
 def pair_kernel(ib, q_ref, lt_ref, kl_ref, r0_ref, r1_ref, w_ref, b_ref, *rest):
@@ -321,10 +333,11 @@
     xs = [shift(v, "x", -away) for v, away in zip(xs, RING[1:])]
     near0, near1, l = join_near(l, first, second, xs, ring(second, "z")[1:])
     l = lax.ppermute(l, ("z", "rep"), [(z * 4 + y, y * 4 + z) for z in range(4) for y in range(4)])
+    near0, l = lax.optimization_barrier((near0, l))
     sides0 = [shift(near0, "z", 1), shift(near0, "z", -1)]
     sides1 = [shift(near1, "x", 1), shift(near1, "x", -1)]
-    l = lax.optimization_barrier((l, *sides0, *sides1))[0]
-    lt, kl, wt, bt = arrange_left(ring(l, "rep"), wf, bf.reshape(1, -1))
+    wt, bt = arrange_weights(wf, bf.reshape(1, -1), near0)
+    lt, kl = arrange_left(ring(l, "rep"))
     own = join_far(ring_onward(near0, *sides0, "z") + ring_onward(near1, *sides1, "x"), kl)
     other = [swap(v) for v in own]
     out = pair_block(core.astype(jnp.int32).reshape(1), lt, kl, own, wt, bt, None)

time: 111 us -> 110 us (level)
  waiting for transfers between devices: 36.6 us -> 20.9 us
  starting transfers between devices: 25.5 us -> 40.7 us
    ppermute x17, waiting for transfers between devices: 34.8 us -> 19.2 us  [shift(): return lax.ppermute(v, axis, [(i, (i + by) % 4) for i in range(4)])]
    ppermute x17, starting transfers between devices: 24.3 us -> 39.5 us  [shift(): return lax.ppermute(v, axis, [(i, (i + by) % 4) for i in range(4)])]
  transfers between devices with their start and end apart: 21 -> 21, of which waited for: 10 -> 8; matrix products, arithmetic and copies ran while one was open for 0% -> 0% of each run, Pallas kernels for 18% -> 18%
where the time goes in v3:
time: 110 us; the launch traced here: 109 us
  Pallas kernels  44.2 us (40%)
  starting transfers between devices  40.7 us (37%)
  waiting for transfers between devices  20.9 us (19%)
  local copies, waits for them, and re-layouts  2.64 us (2%)
    ppermute x17, starting transfers between devices, shift(): return lax.ppermute(v, axis, [(i, (i + by) % 4) for i in range(4)])  39.5 us
    pallas_call x2, Pallas kernels, pair_block(): pl.pallas_call(functools.partial(pair_kernel, ib), grid_spec=pltpu.Prefet...  33.1 us
    ppermute x17, waiting for transfers between devices, shift(): return lax.ppermute(v, axis, [(i, (i + by) % 4) for i in range(4)])  19.2 us
    pallas_call x1, Pallas kernels, prepare(): pl.pallas_call(prepare_kernel, grid_spec=pltpu.PrefetchScalarGridSpec(num...  5.67 us
    pallas_call x1, Pallas kernels, arrange_left(): pl.pallas_call(left_kernel, out_shape=[jax.ShapeDtypeStruct((2, ROWS * FE...  3.06 us
    unnamed x10, local copies, waits for them, and re-layouts  2.56 us
  transfers between devices with their start and end apart: 21, of which 8 were waited for; matrix products, arithmetic and copies ran while one was open for 0% of the time, Pallas kernels for 18%

profile of v3, /device:TPU:0, one launch (start us, length us, event | category | flops | bytes accessed | tf_op | source)
XLA Modules:
  0.0 108.5 jit_solution(9486649840213194052)
XLA Ops:
  0.0 5.7 %prepare.1 = (bf16[8,17408]{1,0:T(8,128)(2,1)}, bf16[8,17408]{1,0:T(8,128)(2,1)}) custom-call(s32[1]{0:T(128)} %bitcast.1.rep_ref, bf16[8,512,256]{2,1,0:T(8,128)(2,1)} %x_ref.1, bf16[8,512]{1,0:T(8,128)(2,1)} %pres_ref.1, s32[1,2048]{1,0:T(1,128)} %bitcast.14, f32[1,256]{1,0:T(1,128)} %bitcast.15, f32[1,256]{1,0:T(1,128)} %bitcast.16, ...), custom_call_target="tpu_custom_call" | custom-call | flops 140000000 | bytes 3145728 | tf_op jit(solution)/shard_map/prepare/pallas_call | solution.py:84
  5.7 0.0 collective-permute-start
  5.7 1.8 %collective-permute-done.got_ref = bf16[8,17408]{1,0:T(8,128)(2,1)S(1)} collective-permute-done((bf16[8,17408]{1,0:T(8,128)(2,1)}, bf16[8,17408]{1,0:T(8,128)(2,1)S(1)}, u32[]{:S(2)}, u32[]{:S(2)}) %collective-permute-start) | collective-permute-done | bytes 278560 | tf_op jit(solution)/shard_map/ppermute | solution.py:331
  7.4 0.0 copy-start
  7.4 1.0 copy-done
  8.4 0.1 split.1
  8.5 4.1 %collective-permute-start.6 = (bf16[16,4352]{1,0:T(8,128)(2,1)S(1)}, bf16[16,4352]{1,0:T(8,128)(2,1)S(1)}, u32[]{:S(2)}, u32[]{:S(2)}) collective-permute-start(bf16[16,4352]{1,0:T(8,128)(2,1)S(1)} %get-tuple-element.28.second_ref), channel_id=1, source_target_pairs={{0,64},{32,96},{64,0},{96,32},{1,65},{33,97},{65,1},{97,33},{2,66}... | collective-permute-start | bytes 417800 | tf_op jit(solution)/shard_map/ppermute | solution.py:305
  12.6 1.5 %collective-permute-start.1 = (bf16[16,6528]{1,0:T(8,128)(2,1)S(1)}, bf16[16,6528]{1,0:T(8,128)(2,1)S(1)}, u32[]{:S(2)}, u32[]{:S(2)}) collective-permute-start(bf16[16,6528]{1,0:T(8,128)(2,1)S(1)} %get-tuple-element.29), channel_id=1, source_target_pairs={{0,8},{8,16},{16,24},{24,0},{1,9},{9,17},{17,25},{25,1},{2,10},{10... | collective-permute-start | bytes 626696 | tf_op jit(solution)/shard_map/ppermute | solution.py:305
  14.1 1.7 %collective-permute-start.2 = (bf16[16,6528]{1,0:T(8,128)(2,1)S(1)}, bf16[16,6528]{1,0:T(8,128)(2,1)S(1)}, u32[]{:S(2)}, u32[]{:S(2)}) collective-permute-start(bf16[16,6528]{1,0:T(8,128)(2,1)S(1)} %get-tuple-element.30), channel_id=1, source_target_pairs={{0,24},{8,0},{16,8},{24,16},{1,25},{9,1},{17,9},{25,17},{2,26},{10... | collective-permute-start | bytes 626696 | tf_op jit(solution)/shard_map/ppermute | solution.py:305
  15.8 1.8 %collective-permute-start.3 = (bf16[16,6528]{1,0:T(8,128)(2,1)S(1)}, bf16[16,6528]{1,0:T(8,128)(2,1)S(1)}, u32[]{:S(2)}, u32[]{:S(2)}) collective-permute-start(bf16[16,6528]{1,0:T(8,128)(2,1)S(1)} %get-tuple-element.31), channel_id=1, source_target_pairs={{0,16},{8,24},{16,0},{24,8},{1,17},{9,25},{17,1},{25,9},{2,18},{10... | collective-permute-start | bytes 626696 | tf_op jit(solution)/shard_map/ppermute | solution.py:305
  17.6 0.7 collective-permute-start.5
  18.4 0.0 collective-permute-done.6.refs_5_
  18.4 1.3 %collective-permute-start.4 = (bf16[16,4352]{1,0:T(8,128)(2,1)S(1)}, bf16[16,4352]{1,0:T(8,128)(2,1)S(1)}, u32[]{:S(2)}, u32[]{:S(2)}) collective-permute-start(bf16[16,4352]{1,0:T(8,128)(2,1)S(1)} %get-tuple-element.28.second_ref), channel_id=1, source_target_pairs={{0,32},{32,64},{64,96},{96,0},{1,33},{33,65},{65,97},{97,1},{2,34}... | collective-permute-start | bytes 417800 | tf_op jit(solution)/shard_map/ppermute | solution.py:305
  19.7 3.0 %collective-permute-done.5.refs_4_ = bf16[16,4352]{1,0:T(8,128)(2,1)S(1)} collective-permute-done((bf16[16,4352]{1,0:T(8,128)(2,1)S(1)}, bf16[16,4352]{1,0:T(8,128)(2,1)S(1)}, u32[]{:S(2)}, u32[]{:S(2)}) %collective-permute-start.5) | collective-permute-done | bytes 139296 | tf_op jit(solution)/shard_map/ppermute | solution.py:305
  22.7 1.9 %collective-permute-done.4.refs_3_ = bf16[16,4352]{1,0:T(8,128)(2,1)S(1)} collective-permute-done((bf16[16,4352]{1,0:T(8,128)(2,1)S(1)}, bf16[16,4352]{1,0:T(8,128)(2,1)S(1)}, u32[]{:S(2)}, u32[]{:S(2)}) %collective-permute-start.4) | collective-permute-done | bytes 139296 | tf_op jit(solution)/shard_map/ppermute | solution.py:305
  24.6 0.0 collective-permute-done.1.refs_0_
  24.6 0.0 collective-permute-done.2.refs_1_
  24.6 1.6 %collective-permute-done.3.refs_2_ = bf16[16,6528]{1,0:T(8,128)(2,1)S(1)} collective-permute-done((bf16[16,6528]{1,0:T(8,128)(2,1)S(1)}, bf16[16,6528]{1,0:T(8,128)(2,1)S(1)}, u32[]{:S(2)}, u32[]{:S(2)}) %collective-permute-start.3) | collective-permute-done | bytes 208928 | tf_op jit(solution)/shard_map/ppermute | solution.py:305
  26.2 0.1 join_near.1
  26.3 0.7 collective-permute-start.7
  27.0 2.0 %collective-permute-start.16 = (bf16[64,4352]{1,0:T(8,128)(2,1)S(1)}, bf16[64,4352]{1,0:T(8,128)(2,1)S(1)}, u32[]{:S(2)}, u32[]{:S(2)}) collective-permute-start(bf16[64,4352]{1,0:T(8,128)(2,1)S(1)} %get-tuple-element.38.refs_5_), channel_id=1, source_target_pairs={{0,24},{8,0},{16,8},{24,16},{1,25},{9,1},{17,9},{25,17},{2,26},{10... | collective-permute-start | bytes 1671176 | tf_op jit(solution)/shard_map/ppermute | solution.py:305
  29.0 0.1 collective-permute-start.15
  29.1 0.0 collective-permute-done.7.l0_ref
  29.1 16.7 %collective-permute-start.12 = (bf16[64,4352]{1,0:T(8,128)(2,1)S(1)}, bf16[64,4352]{1,0:T(8,128)(2,1)S(1)}, u32[]{:S(2)}, u32[]{:S(2)}) collective-permute-start(bf16[64,4352]{1,0:T(8,128)(2,1)S(1)} %get-tuple-element.37.refs_0_.after_ref), channel_id=1, source_target_pairs={{0,96},{32,0},{64,32},{96,64},{1,97},{33,1},{65,33},{97,65},{2,98}... | collective-permute-start | bytes 1671176 | tf_op jit(solution)/shard_map/ppermute | solution.py:305
  45.7 0.0 collective-permute-start.11
  45.7 2.3 %collective-permute-start.10 = (bf16[64,2176]{1,0:T(8,128)(2,1)S(1)}, bf16[64,2176]{1,0:T(8,128)(2,1)S(1)}, u32[]{:S(2)}, u32[]{:S(2)}) collective-permute-start(bf16[64,2176]{1,0:T(8,128)(2,1)S(1)} %collective-permute-done.7.l0_ref), channel_id=1, source_target_pairs={{0,2},{1,3},{2,0},{3,1},{4,6},{5,7},{6,4},{7,5},{8,10},{9,11},{10,... | collective-permute-start | bytes 835592 | tf_op jit(solution)/shard_map/ppermute | solution.py:305
  48.1 0.0 collective-permute-done.16.refs_7_
  48.1 2.0 %collective-permute-start.9 = (bf16[64,2176]{1,0:T(8,128)(2,1)S(1)}, bf16[64,2176]{1,0:T(8,128)(2,1)S(1)}, u32[]{:S(2)}, u32[]{:S(2)}) collective-permute-start(bf16[64,2176]{1,0:T(8,128)(2,1)S(1)} %collective-permute-done.7.l0_ref), channel_id=1, source_target_pairs={{0,3},{1,0},{2,1},{3,2},{4,7},{5,4},{6,5},{7,6},{8,11},{9,8},{10,9... | collective-permute-start | bytes 835592 | tf_op jit(solution)/shard_map/ppermute | solution.py:305
  50.1 0.0 collective-permute-done.15.refs_6_
  50.1 0.9 collective-permute-start.8
  51.1 6.4 %collective-permute-done.12.refs_2_ = bf16[64,4352]{1,0:T(8,128)(2,1)S(1)} collective-permute-done((bf16[64,4352]{1,0:T(8,128)(2,1)S(1)}, bf16[64,4352]{1,0:T(8,128)(2,1)S(1)}, u32[]{:S(2)}, u32[]{:S(2)}) %collective-permute-start.12) | collective-permute-done | bytes 557088 | tf_op jit(solution)/shard_map/ppermute | solution.py:305
  57.5 1.4 %collective-permute-start.18 = (bf16[64,2176]{1,0:T(8,128)(2,1)S(1)}, bf16[64,2176]{1,0:T(8,128)(2,1)S(1)}, u32[]{:S(2)}, u32[]{:S(2)}) collective-permute-start(bf16[64,2176]{1,0:T(8,128)(2,1)S(1)} %slice.19), channel_id=1, source_target_pairs={{0,24},{8,0},{16,8},{24,16},{1,25},{9,1},{17,9},{25,17},{2,26},{10... | collective-permute-start | bytes 835592 | tf_op jit(solution)/shard_map/ppermute | solution.py:305
  58.9 2.0 %collective-permute-done.11.refs_1_ = bf16[64,4352]{1,0:T(8,128)(2,1)S(1)} collective-permute-done((bf16[64,4352]{1,0:T(8,128)(2,1)S(1)}, bf16[64,4352]{1,0:T(8,128)(2,1)S(1)}, u32[]{:S(2)}, u32[]{:S(2)}) %collective-permute-start.11) | collective-permute-done | bytes 557088 | tf_op jit(solution)/shard_map/ppermute | solution.py:305
  60.9 0.8 collective-permute-start.17
  61.7 0.0 collective-permute-done.10.l3_ref
  61.7 1.7 %collective-permute-start.14 = (bf16[64,2176]{1,0:T(8,128)(2,1)S(1)}, bf16[64,2176]{1,0:T(8,128)(2,1)S(1)}, u32[]{:S(2)}, u32[]{:S(2)}) collective-permute-start(bf16[64,2176]{1,0:T(8,128)(2,1)S(1)} %slice.17), channel_id=1, source_target_pairs={{0,96},{32,0},{64,32},{96,64},{1,97},{33,1},{65,33},{97,65},{2,98}... | collective-permute-start | bytes 835592 | tf_op jit(solution)/shard_map/ppermute | solution.py:305
  63.4 0.0 collective-permute-done.9.l2_ref
  63.4 0.4 collective-permute-start.13
  63.8 0.0 collective-permute-done.8.l1_ref
  63.8 3.1 %arrange_left.1 = (bf16[2,2048,256]{2,1,0:T(8,128)(2,1)S(1)}, bf16[64,256]{1,0:T(8,128)(2,1)S(1)}) custom-call(bf16[64,2176]{1,0:T(8,128)(2,1)S(1)} %collective-permute-done.7.l0_ref, bf16[64,2176]{1,0:T(8,128)(2,1)S(1)} %collective-permute-done.8.l1_ref, bf16[64,2176]{1,0:T(8,128)(2,1)S(1)} %collective-permute-done.9.l2_ref, ...), custom_call_target="tpu_custom_call" | custom-call | flops 1000000 | bytes 3145728 | tf_op jit(solution)/shard_map/arrange_left/pallas_call | solution.py:209
  66.9 0.0 copy-start.3
  66.9 0.0 collective-permute-done.18.refs_9_
  66.9 2.2 %collective-permute-done.17.refs_8_ = bf16[64,2176]{1,0:T(8,128)(2,1)S(1)} collective-permute-done((bf16[64,2176]{1,0:T(8,128)(2,1)S(1)}, bf16[64,2176]{1,0:T(8,128)(2,1)S(1)}, u32[]{:S(2)}, u32[]{:S(2)}) %collective-permute-start.17) | collective-permute-done | bytes 278560 | tf_op jit(solution)/shard_map/ppermute | solution.py:305
  69.1 0.0 collective-permute-done.14.refs_4_
  69.1 2.0 %collective-permute-done.13.refs_3_ = bf16[64,2176]{1,0:T(8,128)(2,1)S(1)} collective-permute-done((bf16[64,2176]{1,0:T(8,128)(2,1)S(1)}, bf16[64,2176]{1,0:T(8,128)(2,1)S(1)}, u32[]{:S(2)}, u32[]{:S(2)}) %collective-permute-start.13) | collective-permute-done | bytes 278560 | tf_op jit(solution)/shard_map/ppermute | solution.py:305
  71.2 0.0 copy-start.1
  71.2 0.0 copy-start.2
  71.2 1.7 %join_far.1 = (bf16[256,4352]{1,0:T(8,128)(2,1)}, bf16[256,4352]{1,0:T(8,128)(2,1)S(1)}) custom-call(bf16[64,256]{1,0:T(8,128)(2,1)S(1)} %get-tuple-element.36.after_ref.kl_ref, bf16[64,4352]{1,0:T(8,128)(2,1)S(1)} %get-tuple-element.37.refs_0_.after_ref, bf16[64,4352]{1,0:T(8,128)(2,1)S(1)} %collective-permute-done.11.refs_1_, ...), custom_call_target="tpu_custom_call" | custom-call | bytes 8388608 | tf_op jit(solution)/shard_map/join_far/pallas_call | solution.py:179
  72.9 0.0 copy-done.3
  72.9 0.0 collective-permute-start.19
  72.9 0.5 collective-permute-start.20
  73.4 0.0 copy-done.1
  73.4 0.0 copy-done.2
  73.4 0.4 arrange_weights.1
  73.8 0.0 copy-start.4
  73.8 1.6 %copy-done.4 = bf16[2,2048,256]{2,1,0:T(8,128)(2,1)S(1)} copy-done((bf16[2,2048,256]{2,1,0:T(8,128)(2,1)S(1)}, bf16[2,2048,256]{2,1,0:T(8,128)(2,1)}, u32[]{:S(2)}) %copy-start.4) | copy-done | bytes 2097176
  75.4 16.3 %pair_block.2.rest_0_ = bf16[64,512,128]{2,1,0:T(8,128)(2,1)} custom-call(s32[1]{0:T(128)} %bitcast.10.q_ref, bf16[2,2048,256]{2,1,0:T(8,128)(2,1)S(1)} %copy-done.4, bf16[64,256]{1,0:T(8,128)(2,1)S(1)} %get-tuple-element.36.after_ref.kl_ref, bf16[256,4352]{1,0:T(8,128)(2,1)} %get-tuple-element.39.r0_ref, bf16[256,4352]{1,0:T(8,128)(2,1)S(1)} %get-tuple-element.40.r1_ref, ...), custom_call_target="tpu_custom_call" | custom-call | flops 12884901888 | bytes 12582912 | tf_op jit(solution)/shard_map/pair_block/pallas_call | solution.py:282
  91.7 0.0 collective-permute-done.19.r0_ref
  91.7 0.0 collective-permute-done.20.r1_ref
  91.7 16.8 %pair_block.3 = bf16[64,512,128]{2,1,0:T(8,128)(2,1)} custom-call(s32[1]{0:T(128)} %bitcast.q_ref, bf16[2,2048,256]{2,1,0:T(8,128)(2,1)S(1)} %copy-done.4, bf16[64,256]{1,0:T(8,128)(2,1)S(1)} %get-tuple-element.36.after_ref.kl_ref, bf16[256,4352]{1,0:T(8,128)(2,1)} %collective-permute-done.19.r0_ref, ...), custom_call_target="tpu_custom_call", output_to_operand_aliasing={{}: (7, {})} | custom-call | flops 12884901888 | bytes 12582912 | tf_op jit(solution)/shard_map/pair_block/pallas_call | solution.py:282
  (4 shorter events, 0.1 us)
Async XLA Ops:
  5.7 1.8 %collective-permute-start = (bf16[8,17408]{1,0:T(8,128)(2,1)}, bf16[8,17408]{1,0:T(8,128)(2,1)S(1)}, u32[]{:S(2)}, u32[]{:S(2)}) collective-permute-start(bf16[8,17408]{1,0:T(8,128)(2,1)} %get-tuple-element.25), channel_id=1, source_target_pairs={{0,4},{4,0},{1,5},{5,1},{2,6},{6,2},{3,7},{7,3},{8,12},{12,8},{9,1... | collective-permute-start | bytes 835592 | tf_op jit(solution)/shard_map/ppermute | solution.py:331
  7.4 1.0 copy-start
  8.5 9.8 %collective-permute-start.6 = (bf16[16,4352]{1,0:T(8,128)(2,1)S(1)}, bf16[16,4352]{1,0:T(8,128)(2,1)S(1)}, u32[]{:S(2)}, u32[]{:S(2)}) collective-permute-start(bf16[16,4352]{1,0:T(8,128)(2,1)S(1)} %get-tuple-element.28.second_ref), channel_id=1, source_target_pairs={{0,64},{32,96},{64,0},{96,32},{1,65},{33,97},{65,1},{97,33},{2,66}... | collective-permute-start | bytes 417800 | tf_op jit(solution)/shard_map/ppermute | solution.py:305
  12.6 12.0 %collective-permute-start.1 = (bf16[16,6528]{1,0:T(8,128)(2,1)S(1)}, bf16[16,6528]{1,0:T(8,128)(2,1)S(1)}, u32[]{:S(2)}, u32[]{:S(2)}) collective-permute-start(bf16[16,6528]{1,0:T(8,128)(2,1)S(1)} %get-tuple-element.29), channel_id=1, source_target_pairs={{0,8},{8,16},{16,24},{24,0},{1,9},{9,17},{17,25},{25,1},{2,10},{10... | collective-permute-start | bytes 626696 | tf_op jit(solution)/shard_map/ppermute | solution.py:305
  14.1 10.6 %collective-permute-start.2 = (bf16[16,6528]{1,0:T(8,128)(2,1)S(1)}, bf16[16,6528]{1,0:T(8,128)(2,1)S(1)}, u32[]{:S(2)}, u32[]{:S(2)}) collective-permute-start(bf16[16,6528]{1,0:T(8,128)(2,1)S(1)} %get-tuple-element.30), channel_id=1, source_target_pairs={{0,24},{8,0},{16,8},{24,16},{1,25},{9,1},{17,9},{25,17},{2,26},{10... | collective-permute-start | bytes 626696 | tf_op jit(solution)/shard_map/ppermute | solution.py:305
  15.8 10.4 %collective-permute-start.3 = (bf16[16,6528]{1,0:T(8,128)(2,1)S(1)}, bf16[16,6528]{1,0:T(8,128)(2,1)S(1)}, u32[]{:S(2)}, u32[]{:S(2)}) collective-permute-start(bf16[16,6528]{1,0:T(8,128)(2,1)S(1)} %get-tuple-element.31), channel_id=1, source_target_pairs={{0,16},{8,24},{16,0},{24,8},{1,17},{9,25},{17,1},{25,9},{2,18},{10... | collective-permute-start | bytes 626696 | tf_op jit(solution)/shard_map/ppermute | solution.py:305
  17.6 5.1 %collective-permute-start.5 = (bf16[16,4352]{1,0:T(8,128)(2,1)S(1)}, bf16[16,4352]{1,0:T(8,128)(2,1)S(1)}, u32[]{:S(2)}, u32[]{:S(2)}) collective-permute-start(bf16[16,4352]{1,0:T(8,128)(2,1)S(1)} %get-tuple-element.28.second_ref), channel_id=1, source_target_pairs={{0,96},{32,0},{64,32},{96,64},{1,97},{33,1},{65,33},{97,65},{2,98}... | collective-permute-start | bytes 417800 | tf_op jit(solution)/shard_map/ppermute | solution.py:305
  18.4 6.3 %collective-permute-start.4 = (bf16[16,4352]{1,0:T(8,128)(2,1)S(1)}, bf16[16,4352]{1,0:T(8,128)(2,1)S(1)}, u32[]{:S(2)}, u32[]{:S(2)}) collective-permute-start(bf16[16,4352]{1,0:T(8,128)(2,1)S(1)} %get-tuple-element.28.second_ref), channel_id=1, source_target_pairs={{0,32},{32,64},{64,96},{96,0},{1,33},{33,65},{65,97},{97,1},{2,34}... | collective-permute-start | bytes 417800 | tf_op jit(solution)/shard_map/ppermute | solution.py:305
  26.3 2.8 %collective-permute-start.7 = (bf16[64,2176]{1,0:T(8,128)(2,1)S(1)}, bf16[64,2176]{1,0:T(8,128)(2,1)S(1)}, u32[]{:S(2)}, u32[]{:S(2)}) collective-permute-start(bf16[64,2176]{1,0:T(8,128)(2,1)S(1)} %get-tuple-element.33), channel_id=1, source_target_pairs={{0,0},{1,32},{2,64},{3,96},{32,1},{33,33},{34,65},{35,97},{64,2},{... | collective-permute-start | bytes 835592 | tf_op jit(solution)/shard_map/ppermute | solution.py:335
  27.0 21.1 %collective-permute-start.16 = (bf16[64,4352]{1,0:T(8,128)(2,1)S(1)}, bf16[64,4352]{1,0:T(8,128)(2,1)S(1)}, u32[]{:S(2)}, u32[]{:S(2)}) collective-permute-start(bf16[64,4352]{1,0:T(8,128)(2,1)S(1)} %get-tuple-element.38.refs_5_), channel_id=1, source_target_pairs={{0,24},{8,0},{16,8},{24,16},{1,25},{9,1},{17,9},{25,17},{2,26},{10... | collective-permute-start | bytes 1671176 | tf_op jit(solution)/shard_map/ppermute | solution.py:305
  29.0 21.1 %collective-permute-start.15 = (bf16[64,4352]{1,0:T(8,128)(2,1)S(1)}, bf16[64,4352]{1,0:T(8,128)(2,1)S(1)}, u32[]{:S(2)}, u32[]{:S(2)}) collective-permute-start(bf16[64,4352]{1,0:T(8,128)(2,1)S(1)} %get-tuple-element.38.refs_5_), channel_id=1, source_target_pairs={{0,8},{8,16},{16,24},{24,0},{1,9},{9,17},{17,25},{25,1},{2,10},{10... | collective-permute-start | bytes 1671176 | tf_op jit(solution)/shard_map/ppermute | solution.py:305
  29.1 28.4 %collective-permute-start.12 = (bf16[64,4352]{1,0:T(8,128)(2,1)S(1)}, bf16[64,4352]{1,0:T(8,128)(2,1)S(1)}, u32[]{:S(2)}, u32[]{:S(2)}) collective-permute-start(bf16[64,4352]{1,0:T(8,128)(2,1)S(1)} %get-tuple-element.37.refs_0_.after_ref), channel_id=1, source_target_pairs={{0,96},{32,0},{64,32},{96,64},{1,97},{33,1},{65,33},{97,65},{2,98}... | collective-permute-start | bytes 1671176 | tf_op jit(solution)/shard_map/ppermute | solution.py:305
  45.7 15.1 %collective-permute-start.11 = (bf16[64,4352]{1,0:T(8,128)(2,1)S(1)}, bf16[64,4352]{1,0:T(8,128)(2,1)S(1)}, u32[]{:S(2)}, u32[]{:S(2)}) collective-permute-start(bf16[64,4352]{1,0:T(8,128)(2,1)S(1)} %get-tuple-element.37.refs_0_.after_ref), channel_id=1, source_target_pairs={{0,32},{32,64},{64,96},{96,0},{1,33},{33,65},{65,97},{97,1},{2,34}... | collective-permute-start | bytes 1671176 | tf_op jit(solution)/shard_map/ppermute | solution.py:305
  45.7 16.0 %collective-permute-start.10 = (bf16[64,2176]{1,0:T(8,128)(2,1)S(1)}, bf16[64,2176]{1,0:T(8,128)(2,1)S(1)}, u32[]{:S(2)}, u32[]{:S(2)}) collective-permute-start(bf16[64,2176]{1,0:T(8,128)(2,1)S(1)} %collective-permute-done.7.l0_ref), channel_id=1, source_target_pairs={{0,2},{1,3},{2,0},{3,1},{4,6},{5,7},{6,4},{7,5},{8,10},{9,11},{10,... | collective-permute-start | bytes 835592 | tf_op jit(solution)/shard_map/ppermute | solution.py:305
  48.1 15.3 %collective-permute-start.9 = (bf16[64,2176]{1,0:T(8,128)(2,1)S(1)}, bf16[64,2176]{1,0:T(8,128)(2,1)S(1)}, u32[]{:S(2)}, u32[]{:S(2)}) collective-permute-start(bf16[64,2176]{1,0:T(8,128)(2,1)S(1)} %collective-permute-done.7.l0_ref), channel_id=1, source_target_pairs={{0,3},{1,0},{2,1},{3,2},{4,7},{5,4},{6,5},{7,6},{8,11},{9,8},{10,9... | collective-permute-start | bytes 835592 | tf_op jit(solution)/shard_map/ppermute | solution.py:305
  50.1 13.7 %collective-permute-start.8 = (bf16[64,2176]{1,0:T(8,128)(2,1)S(1)}, bf16[64,2176]{1,0:T(8,128)(2,1)S(1)}, u32[]{:S(2)}, u32[]{:S(2)}) collective-permute-start(bf16[64,2176]{1,0:T(8,128)(2,1)S(1)} %collective-permute-done.7.l0_ref), channel_id=1, source_target_pairs={{0,1},{1,2},{2,3},{3,0},{4,5},{5,6},{6,7},{7,4},{8,9},{9,10},{10,1... | collective-permute-start | bytes 835592 | tf_op jit(solution)/shard_map/ppermute | solution.py:305
  57.5 9.5 %collective-permute-start.18 = (bf16[64,2176]{1,0:T(8,128)(2,1)S(1)}, bf16[64,2176]{1,0:T(8,128)(2,1)S(1)}, u32[]{:S(2)}, u32[]{:S(2)}) collective-permute-start(bf16[64,2176]{1,0:T(8,128)(2,1)S(1)} %slice.19), channel_id=1, source_target_pairs={{0,24},{8,0},{16,8},{24,16},{1,25},{9,1},{17,9},{25,17},{2,26},{10... | collective-permute-start | bytes 835592 | tf_op jit(solution)/shard_map/ppermute | solution.py:305
  60.9 8.3 %collective-permute-start.17 = (bf16[64,2176]{1,0:T(8,128)(2,1)S(1)}, bf16[64,2176]{1,0:T(8,128)(2,1)S(1)}, u32[]{:S(2)}, u32[]{:S(2)}) collective-permute-start(bf16[64,2176]{1,0:T(8,128)(2,1)S(1)} %slice.18), channel_id=1, source_target_pairs={{0,8},{8,16},{16,24},{24,0},{1,9},{9,17},{17,25},{25,1},{2,10},{10... | collective-permute-start | bytes 835592 | tf_op jit(solution)/shard_map/ppermute | solution.py:305
  61.7 7.4 %collective-permute-start.14 = (bf16[64,2176]{1,0:T(8,128)(2,1)S(1)}, bf16[64,2176]{1,0:T(8,128)(2,1)S(1)}, u32[]{:S(2)}, u32[]{:S(2)}) collective-permute-start(bf16[64,2176]{1,0:T(8,128)(2,1)S(1)} %slice.17), channel_id=1, source_target_pairs={{0,96},{32,0},{64,32},{96,64},{1,97},{33,1},{65,33},{97,65},{2,98}... | collective-permute-start | bytes 835592 | tf_op jit(solution)/shard_map/ppermute | solution.py:305
  63.4 7.8 %collective-permute-start.13 = (bf16[64,2176]{1,0:T(8,128)(2,1)S(1)}, bf16[64,2176]{1,0:T(8,128)(2,1)S(1)}, u32[]{:S(2)}, u32[]{:S(2)}) collective-permute-start(bf16[64,2176]{1,0:T(8,128)(2,1)S(1)} %slice.16), channel_id=1, source_target_pairs={{0,32},{32,64},{64,96},{96,0},{1,33},{33,65},{65,97},{97,1},{2,34}... | collective-permute-start | bytes 835592 | tf_op jit(solution)/shard_map/ppermute | solution.py:305
  66.9 6.0 %copy-start.3 = (bf16[2,2048,256]{2,1,0:T(8,128)(2,1)}, bf16[2,2048,256]{2,1,0:T(8,128)(2,1)S(1)}, u32[]{:S(2)}) copy-start(bf16[2,2048,256]{2,1,0:T(8,128)(2,1)S(1)} %get-tuple-element.35.lt_ref) | copy-start | bytes 6291460
  71.2 2.2 %copy-start.1 = (bf16[1024,128]{1,0:T(8,128)(2,1)S(1)}, bf16[1024,128]{1,0:T(8,128)(2,1)}, u32[]{:S(2)}) copy-start(bf16[1024,128]{1,0:T(8,128)(2,1)} %wf_ref.1) | copy-start | bytes 786436
  71.2 2.2 %copy-start.2 = (f32[128]{0:T(128)S(1)}, f32[128]{0:T(128)}, u32[]{:S(2)}) copy-start(f32[128]{0:T(128)} %param.21) | copy-start | bytes 1540
  72.9 18.8 %collective-permute-start.19 = (bf16[256,4352]{1,0:T(8,128)(2,1)}, bf16[256,4352]{1,0:T(8,128)(2,1)}, u32[]{:S(2)}, u32[]{:S(2)}) collective-permute-start(bf16[256,4352]{1,0:T(8,128)(2,1)} %get-tuple-element.39.r0_ref), channel_id=1, source_target_pairs={{0,4},{4,0},{1,5},{5,1},{2,6},{6,2},{3,7},{7,3},{8,12},{12,8},{9,1... | collective-permute-start | bytes 6684680 | tf_op jit(solution)/shard_map/ppermute | solution.py:331
  72.9 18.8 %collective-permute-start.20 = (bf16[256,4352]{1,0:T(8,128)(2,1)S(1)}, bf16[256,4352]{1,0:T(8,128)(2,1)}, u32[]{:S(2)}, u32[]{:S(2)}) collective-permute-start(bf16[256,4352]{1,0:T(8,128)(2,1)S(1)} %get-tuple-element.40.r1_ref), channel_id=1, source_target_pairs={{0,4},{4,0},{1,5},{5,1},{2,6},{6,2},{3,7},{7,3},{8,12},{12,8},{9,1... | collective-permute-start | bytes 6684680 | tf_op jit(solution)/shard_map/ppermute | solution.py:331
  73.8 1.6 %copy-start.4 = (bf16[2,2048,256]{2,1,0:T(8,128)(2,1)S(1)}, bf16[2,2048,256]{2,1,0:T(8,128)(2,1)}, u32[]{:S(2)}) copy-start(bf16[2,2048,256]{2,1,0:T(8,128)(2,1)} %copy-done.3) | copy-start | bytes 6291460
